TPU v7x, 512 devices: a whole 4x8x8 slice. The times are simulated.
512 devices in a mesh: brick: 32 (over x, y_lo, core), slab: 16 (over y_hi, z).
Axes of the slice: x: 4, y: 8 (y_hi: 2, y_lo: 4; y = y_hi * 4 + y_lo), z: 8, core: 2. Of those that a mesh axis runs over, the one named last changes fastest.
Arguments:
- positions: float32 [3, 16, 6144], P(None, 'slab', 'brick'), may hold values from -3 to 3
- types: int32 [16, 6144], P('slab', 'brick'), may hold values from 0 to 1, as said below
- neighbours: int32 [16, 6144, 64], P('slab', 'brick'), may hold values from 0 to 383
- neighbour_count: int32 [16, 6144], P('slab', 'brick'), may hold values from 32 to 64, as said below
- send_index: int32 [16, 6144], P('slab', 'brick'), may hold values from 0 to 191
- cell_x: int32 [16, 6144], P('slab', 'brick'), may hold values from 0 to 7, as said below
- cell_y: int32 [16, 6144], P('slab', 'brick'), may hold values from 0 to 15, as said below
- cell_z: int32 [16, 6144], P('slab', 'brick'), may hold values from 0 to 255, as said below
- spline_fraction: float32 [3, 16, 6144], P(None, 'slab', 'brick'), may hold values from 0 to 1
- embed_first: float32 [2, 25], replicated, may hold values from -4 to 4
- embed_second: float32 [25, 50], replicated, may hold values from -1.25 to 1.25
- embed_third: float32 [50, 100], replicated, may hold values from -0.875 to 0.875
- energy_in: float32 [1600, 240], replicated, may hold values from -0.3125 to 0.3125
- energy_hidden: float32 [2, 240, 240], replicated, may hold values from -0.375 to 0.375
- energy_out: float32 [240], replicated, may hold values from -0.375 to 0.375
- wannier_in: float32 [1600, 240], replicated, may hold values from -0.3125 to 0.3125
- wannier_hidden: float32 [2, 240, 240], replicated, may hold values from -0.375 to 0.375
- wannier_out: float32 [240], replicated, may hold values from -0.01953125 to 0.01953125
- charge_base: float32 [2], replicated, may hold values from -2 to 1
Outputs:
- atom_energy: float32 [16, 6144], P('slab', 'brick')
- potential: float32 [256, 256, 256], P('brick', 'slab')
Inputs may be any that keep to these rules, and one draw needn't show every extreme that they name: The first neighbour_count entries of an atom's neighbour row are live, the rest are padding; the first atom of every block has all 64 slots live. `types`: atoms 3k, 3k + 1 and 3k + 2 of a row form one water molecule: one oxygen and two hydrogens. `cell_x`: each hydrogen's first grid point along the first dimension is that of its molecule's oxygen or one further. `cell_y`: each hydrogen's first grid point along the second dimension is that of its molecule's oxygen or one further. `cell_z`: each hydrogen's first grid point along the third dimension is that of its molecule's oxygen or one further.
All inputs are finite; a program needn't handle non-finite values.
Results may differ from a plain program's by a relative error of at most 0.0003.
Values sent between devices are 32-bit elements; how exact they have to be, the bound alone decides.
A program may use at most 64 MiB of HBM per device.

v0:
```python
import math

import jax
import jax.numpy as jnp
from jax import lax
from jax.sharding import PartitionSpec as P

NG = 256
AXIS = 16


HIGH = lax.Precision.HIGHEST


def with_halo(cells, sides, width):
    for axis, dim in sides:
        count = lax.axis_size(axis)
        head = lax.slice_in_dim(cells, 0, width, axis=dim)
        tail = lax.slice_in_dim(cells, cells.shape[dim] - width, cells.shape[dim], axis=dim)
        cells = jnp.concatenate(
            [
                lax.ppermute(tail, axis, [(i, (i + 1) % count) for i in range(count)]),
                cells,
                lax.ppermute(head, axis, [((i + 1) % count, i) for i in range(count)]),
            ],
            axis=dim,
        )
    return cells


def spline_weights(fraction):
    cubed = fraction * fraction * fraction
    square = fraction * fraction
    return jnp.stack(
        [
            (1.0 - fraction) * (1.0 - fraction) * (1.0 - fraction) / 6.0,
            (3.0 * cubed - 6.0 * square + 4.0) / 6.0,
            (-3.0 * cubed + 3.0 * square + 3.0 * fraction + 1.0) / 6.0,
            cubed / 6.0,
        ]
    )


def fitting(descriptor, weight_in, weight_hidden, weight_out):
    hidden = jnp.tanh(jnp.dot(descriptor, weight_in, precision=HIGH))
    for depth_index in range(weight_hidden.shape[0]):
        hidden = jnp.tanh(jnp.dot(hidden, weight_hidden[depth_index], precision=HIGH)) + hidden
    return jnp.dot(hidden, weight_out, precision=HIGH)


def atom_terms(
    extended,
    neighbour_rows,
    neighbour_total,
    embed_first,
    embed_second,
    embed_third,
    energy_in,
    energy_hidden,
    energy_out,
    wannier_in,
    wannier_hidden,
    wannier_out,
):
    atom_count, slots = neighbour_rows.shape
    ghost_rows = (extended.shape[1] - atom_count) // 2
    block_size = 64
    blocks = atom_count // block_size
    present = (jnp.arange(slots, dtype=jnp.int32)[None, :] < neighbour_total[:, None]).astype(
        jnp.float32
    )
    centre_ids = (ghost_rows + jnp.arange(atom_count, dtype=jnp.int32)).reshape(blocks, block_size)
    second_weight = embed_second.T
    third_weight = embed_third.T

    def one_block(pieces):
        centre_rows, rows_block, present_block = pieces
        centre_block = extended[:3, centre_rows]
        gathered = extended[:, rows_block]
        offsets = gathered[:3] - centre_block[:, :, None]
        smooth = present_block / (1.0 + jnp.sum(offsets * offsets, axis=0))
        environment = jnp.stack(
            [smooth, smooth * offsets[0], smooth * offsets[1], smooth * offsets[2]], axis=0
        )
        kind = gathered[3][None]
        mixing = (1.0 - kind) * embed_first[0][:, None, None] + kind * embed_first[1][:, None, None]
        first = jnp.tanh(smooth[None] * mixing).reshape(embed_first.shape[1], block_size * slots)
        second = jnp.tanh(jnp.dot(second_weight, first, precision=HIGH)) + jnp.concatenate(
            [first, first], axis=0
        )
        third = jnp.tanh(jnp.dot(third_weight, second, precision=HIGH)) + jnp.concatenate(
            [second, second], axis=0
        )
        third_blocks = third.reshape(third.shape[0], block_size, slots)
        moments = jnp.einsum("kan,can->akc", third_blocks, environment, precision=HIGH) / slots
        descriptor = jnp.einsum("amc,akc->amk", moments, moments[:, :AXIS], precision=HIGH).reshape(
            block_size, -1
        )
        return (
            fitting(descriptor, energy_in, energy_hidden, energy_out),
            fitting(descriptor, wannier_in, wannier_hidden, wannier_out),
        )

    energy_short, charge_shift = lax.map(
        one_block,
        (
            centre_ids,
            neighbour_rows.reshape(blocks, block_size, slots),
            present.reshape(blocks, block_size, slots),
        ),
    )
    return (energy_short.reshape(atom_count), charge_shift.reshape(atom_count))


def green_table(first, second, third, size):

    def folded(index):
        return jnp.where(index < size // 2, index, index - size).astype(jnp.float32) * (
            2.0 * math.pi / size
        )

    kappa_x = folded(first)[:, None, None]
    kappa_y = folded(second)[None, :, None]
    kappa_z = folded(third)[None, None, :]
    squared = kappa_x * kappa_x + kappa_y * kappa_y + kappa_z * kappa_z
    root = (
        (first[:, None, None] == 0) & (second[None, :, None] == 0) & (third[None, None, :] == 0)
    ).astype(jnp.float32)
    return (1.0 - root) * jnp.exp(-0.5 * squared) / (squared + root)


def dft_tables(size):
    index = jnp.arange(size, dtype=jnp.int32)
    phase = (index[:, None] * index[None, :] % size).astype(jnp.float32) * (2.0 * math.pi / size)
    return (jnp.cos(phase), jnp.sin(phase))


def along(values, table, axis_index):
    result = jnp.tensordot(values, table, axes=([axis_index], [0]), precision=HIGH)
    return jnp.moveaxis(result, -1, axis_index)


def complex_transform(paired, axis_index, cosine, sine, inverse):
    real_part = paired[0]
    imag_part = paired[1]
    inner = axis_index - 1
    real_cos = along(real_part, cosine, inner)
    real_sin = along(real_part, sine, inner)
    imag_cos = along(imag_part, cosine, inner)
    imag_sin = along(imag_part, sine, inner)
    if inverse:
        return jnp.stack([real_cos - imag_sin, imag_cos + real_sin])
    return jnp.stack([real_cos + imag_sin, imag_cos - real_sin])


def fold_windows(values, axis_index, block, count):
    front = jnp.moveaxis(values, axis_index, 0)
    rest = front.shape[1:]
    windows = front.reshape((count, block + 3) + rest)
    main_part = windows[:, :block]
    carried = jnp.roll(windows[:, block:], 1, axis=0)
    main_part = main_part.at[:, :3].add(carried)
    return jnp.moveaxis(main_part.reshape((count * block,) + rest), 0, axis_index)


def make_windows(values, axis_index, block, count):
    front = jnp.moveaxis(values, axis_index, 0)
    rest = front.shape[1:]
    pieces = front.reshape((count, block) + rest)
    trailing = jnp.roll(pieces, -1, axis=0)[:, :3]
    windows = jnp.concatenate([pieces, trailing], axis=1)
    return jnp.moveaxis(windows.reshape((count * (block + 3),) + rest), 0, axis_index)


def spread_matrix(start, weights, width, wrap_size):
    offsets = jnp.arange(4, dtype=jnp.int32)[:, None, None]
    target = start[None, :, None] + offsets
    if wrap_size > 0:
        target = target % wrap_size
    hits = (target == jnp.arange(width, dtype=jnp.int32)[None, None, :]).astype(jnp.float32)
    return jnp.sum(weights[:, :, None] * hits, axis=0)


def per_device(
    positions,
    types,
    neighbours,
    neighbour_count,
    send_index,
    cell_x,
    cell_y,
    cell_z,
    spline_fraction,
    embed_first,
    embed_second,
    embed_third,
    energy_in,
    energy_hidden,
    energy_out,
    wannier_in,
    wannier_hidden,
    wannier_out,
    charge_base,
):
    atom_count = types.shape[1]
    ghost_rows = send_index.shape[1] // 2
    kind_float = types[0].astype(jnp.float32)
    own_atoms = jnp.concatenate([positions[:, 0], kind_float[None]], axis=0)
    outgoing = own_atoms[:, send_index[0]]
    padded_ghosts = with_halo(outgoing, (("brick", 1),), ghost_rows)
    extended = jnp.concatenate(
        [padded_ghosts[:, :ghost_rows], own_atoms, padded_ghosts[:, 3 * ghost_rows :]], axis=1
    )
    energy_short, charge_shift = atom_terms(
        extended,
        neighbours[0],
        neighbour_count[0],
        embed_first,
        embed_second,
        embed_third,
        energy_in,
        energy_hidden,
        energy_out,
        wannier_in,
        wannier_hidden,
        wannier_out,
    )
    charge = (1.0 - kind_float) * charge_base[0] + kind_float * charge_base[1] + charge_shift
    count_x = lax.axis_size("brick")
    count_y = lax.axis_size("slab")
    block_x = NG // count_x
    block_y = NG // count_y
    wide_x = block_x + 3
    wide_y = block_y + 3
    spread_x = spread_matrix(cell_x[0], spline_weights(spline_fraction[0, 0]), wide_x, 0)
    spread_y = spread_matrix(cell_y[0], spline_weights(spline_fraction[1, 0]), wide_y, 0)
    spread_z = spread_matrix(cell_z[0], spline_weights(spline_fraction[2, 0]), NG, NG)
    spread_xy = (spread_x[:, :, None] * spread_y[:, None, :]).reshape(atom_count, wide_x * wide_y)
    charge_grid = jnp.einsum(
        "ap,az->pz", spread_xy, charge[:, None] * spread_z, precision=HIGH
    ).reshape(wide_x, wide_y, NG)
    cosine, sine = dft_tables(NG)
    scale = 1.0 / (NG * NG * NG)
    full_index = jnp.arange(NG, dtype=jnp.int32)
    paired = jnp.stack([along(charge_grid, cosine, 2), -along(charge_grid, sine, 2)])
    moved = lax.all_to_all(paired, "slab", split_axis=3, concat_axis=2, tiled=True)
    moved = complex_transform(fold_windows(moved, 2, block_y, count_y), 2, cosine, sine, False)
    moved = lax.all_to_all(moved, "brick", split_axis=2, concat_axis=1, tiled=True)
    moved = complex_transform(fold_windows(moved, 1, block_x, count_x), 1, cosine, sine, False)
    part_y = NG // count_x
    part_z = NG // count_y
    index_y = lax.axis_index("brick") * part_y + jnp.arange(part_y, dtype=jnp.int32)
    index_z = lax.axis_index("slab") * part_z + jnp.arange(part_z, dtype=jnp.int32)
    moved = moved * (green_table(full_index, index_y, index_z, NG) * scale)[None]
    moved = make_windows(complex_transform(moved, 1, cosine, sine, True), 1, block_x, count_x)
    moved = lax.all_to_all(moved, "brick", split_axis=1, concat_axis=2, tiled=True)
    moved = make_windows(complex_transform(moved, 2, cosine, sine, True), 2, block_y, count_y)
    moved = lax.all_to_all(moved, "slab", split_axis=2, concat_axis=3, tiled=True)
    potential_wide = along(moved[0], cosine, 2) - along(moved[1], sine, 2)
    sampled = jnp.einsum(
        "ap,pz->az", spread_xy, potential_wide.reshape(wide_x * wide_y, NG), precision=HIGH
    )
    potential_at = jnp.sum(sampled * spread_z, axis=1)
    atom_energy = energy_short + 0.5 * charge * potential_at
    return (atom_energy[None, :], potential_wide[:block_x, :block_y])


def solution(mesh):
    placed = (
        P(None, "slab", "brick"),
        P("slab", "brick"),
        P("slab", "brick", None),
        P("slab", "brick"),
        P("slab", "brick"),
        P("slab", "brick"),
        P("slab", "brick"),
        P("slab", "brick"),
        P(None, "slab", "brick"),
        P(),
        P(),
        P(),
        P(),
        P(),
        P(),
        P(),
        P(),
        P(),
        P(),
    )
    return jax.shard_map(
        per_device,
        mesh=mesh,
        in_specs=placed,
        out_specs=(P("slab", "brick"), P("brick", "slab", None)),
        check_vma=False,
    )
```

profile of v0, /device:TPU:1, one launch (start us, length us, event | category | flops | bytes accessed | tf_op | source)
XLA Modules:
  0.0 843.6 jit_solution(2530952535138694566)
XLA Ops:
  3.6 8.8 %collective-permute-start.1 = (f32[4,96]{0,1:T(8,128)S(1)}, f32[4,96]{0,1:T(8,128)S(1)}, u32[]{:S(2)}, u32[]{:S(2)}) collective-permute-start(f32[4,96]{0,1:T(8,128)S(1)} %get-tuple-element.233), channel_id=1, source_target_pairs={{16,0},{32,16},{48,32},{64,48},{80,64},{96,80},{112,96},{128,112},... | collective-permute-start | bytes 4616 | tf_op jit(solution)/shard_map/ppermute | solution.py:24
  22.4 2.4 multiply_add_fusion.1
  27.8 486.7 %while.17 = (s32[]{:T(128)}, f32[3,64]{1,0:T(4,128)}, f32[3,64]{1,0:T(4,128)}, f32[3,64,64]{2,0,1:T(4,128)}, s32[3,64,64]{2,1,0:T(8,128)}, /*index=5*/f32[4,384]...) while((s32[]{:T(128)}, f32[3,64]{1,0:T(4,128)}, ...), condition=%wide.region_2.3_spmd, body=%wide.region_0.2_spmd.sunk | while | flops 1100764416 | bytes 27329496 | solution.py:104
  29.4 10.8 %gather_fusion = f32[4096,4]{1,0:T(8,128)S(1)} fusion(f32[4,384]{0,1:T(8,128)S(1)} %get-tuple-element.474, s32[4096]{0:T(1024)S(1)} %broadcast_clamp_fusion.2), kind=kCustom, calls=%fused_computation.clone.1 | custom fusion | bytes 147456 | tf_op jit(solution)/shard_map/while/body/eval_jaxpr/gather | solution.py:79
  41.3 128.2 %while.18 = (s32[]{:T(128)}, f32[4,384]{0,1:T(8,128)S(1)}, s32[64,2]{0,1:T(2,128)S(1)}, f32[64,3]{1,0:T(8,128)S(1)}, s32[]{:T(128)}, /*index=5*/s32[]{:T(128)}) while((s32[]{:T(128)}, f32[4,384]{0,1:T(8,128)S(1)}, s32[64,2]{0,1:T(2,128)S(1)}, f32[64,3]{1,0:T(8,128)S(1)}, s32[]{:T(128)}, /*index=5*/s32[]{:T(128)}) %tuple.87), condition=%wide.while_cond.2, body=%wide.while_body.2.sunk | while | flops 2 | bytes 173 | solution.py:78
  173.2 2.8 fusion.318
  185.1 3.0 convolution_tanh_fusion.11
  191.6 10.8 %gather_fusion = f32[4096,4]{1,0:T(8,128)S(1)} fusion(f32[4,384]{0,1:T(8,128)S(1)} %get-tuple-element.474, s32[4096]{0:T(1024)S(1)} %broadcast_clamp_fusion.2), kind=kCustom, calls=%fused_computation.clone.1 | custom fusion | bytes 147456 | tf_op jit(solution)/shard_map/while/body/eval_jaxpr/gather | solution.py:79
  203.5 128.2 %while.18 = (s32[]{:T(128)}, f32[4,384]{0,1:T(8,128)S(1)}, s32[64,2]{0,1:T(2,128)S(1)}, f32[64,3]{1,0:T(8,128)S(1)}, s32[]{:T(128)}, /*index=5*/s32[]{:T(128)}) while((s32[]{:T(128)}, f32[4,384]{0,1:T(8,128)S(1)}, s32[64,2]{0,1:T(2,128)S(1)}, f32[64,3]{1,0:T(8,128)S(1)}, s32[]{:T(128)}, /*index=5*/s32[]{:T(128)}) %tuple.87), condition=%wide.while_cond.2, body=%wide.while_body.2.sunk | while | flops 2 | bytes 173 | solution.py:78
  335.4 2.8 fusion.318
  347.2 3.0 convolution_tanh_fusion.11
  353.8 10.8 %gather_fusion = f32[4096,4]{1,0:T(8,128)S(1)} fusion(f32[4,384]{0,1:T(8,128)S(1)} %get-tuple-element.474, s32[4096]{0:T(1024)S(1)} %broadcast_clamp_fusion.2), kind=kCustom, calls=%fused_computation.clone.1 | custom fusion | bytes 147456 | tf_op jit(solution)/shard_map/while/body/eval_jaxpr/gather | solution.py:79
  365.6 128.2 %while.18 = (s32[]{:T(128)}, f32[4,384]{0,1:T(8,128)S(1)}, s32[64,2]{0,1:T(2,128)S(1)}, f32[64,3]{1,0:T(8,128)S(1)}, s32[]{:T(128)}, /*index=5*/s32[]{:T(128)}) while((s32[]{:T(128)}, f32[4,384]{0,1:T(8,128)S(1)}, s32[64,2]{0,1:T(2,128)S(1)}, f32[64,3]{1,0:T(8,128)S(1)}, s32[]{:T(128)}, /*index=5*/s32[]{:T(128)}) %tuple.87), condition=%wide.while_cond.2, body=%wide.while_body.2.sunk | while | flops 2 | bytes 173 | solution.py:78
  497.5 2.8 fusion.318
  509.4 3.0 convolution_tanh_fusion.11
  519.5 2.7 copy.190
  522.2 5.5 reshape.891
  527.7 11.5 %all-to-all-start = ((f32[16,1,6688]{2,1,0:T(1,128)}), f32[16,1,6688]{2,1,0:T(1,128)S(1)}, u32[]{:S(2)}, u32[]{:S(2)}) async-start(f32[16,1,6688]{2,1,0:T(1,128)} %reshape.891), calls=%async_computation | async-start | bytes 868352 | tf_op jit(solution)/shard_map/all_to_all | solution.py:246
  539.3 12.9 %all-to-all-done = f32[16,1,6688]{2,1,0:T(1,128)S(1)} async-done(((f32[16,1,6688]{2,1,0:T(1,128)}), f32[16,1,6688]{2,1,0:T(1,128)S(1)}, u32[]{:S(2)}, u32[]{:S(2)}) %all-to-all-start) | async-done | bytes 428064 | tf_op jit(solution)/shard_map/all_to_all | solution.py:246
  554.3 4.7 reshape.892
  559.1 3.3 copy.238
  562.3 2.8 all_to_all.51
  567.0 2.4 slice.287
  570.5 2.6 copy.232
  573.1 4.5 copy.234
  580.6 4.3 copy.196
  584.9 27.2 %scatter-add.6 = f32[16,16,2,11,16]{1,0,4,3,2:T(8,128)S(1)} dynamic-update-slice(f32[16,16,2,11,16]{1,0,4,3,2:T(8,128)S(1)} %bitcast.449, f32[16,3,2,11,16]{1,0,4,3,2:T(8,128)} %copy.196, s32[]{:T(128)} %constant.152.clone.1, s32[]{:T(128)} %constant.152.clone.1, s32[]{:T(128)} %constant.152.clone.1, s32[]{:T(128)} %constant.152.clone.1, s32[]{:T(128)} %constant.152.clone.1) | dynamic-update-slice | bytes 135172 | tf_op jit(solution)/shard_map/scatter-add | solution.py:162
  618.7 2.6 copy.197
  621.3 4.6 reshape.893
  625.9 11.7 %all-to-all-start.1 = ((f32[32,1,2816]{2,1,0:T(1,128)}), f32[32,1,2816]{2,1,0:T(1,128)S(1)}, u32[]{:S(2)}, u32[]{:S(2)}) async-start(f32[32,1,2816]{2,1,0:T(1,128)} %reshape.893), calls=%async_computation.1 | async-start | bytes 720896 | tf_op jit(solution)/shard_map/all_to_all | solution.py:248
  637.9 12.9 %all-to-all-done.1 = f32[32,1,2816]{2,1,0:T(1,128)S(1)} async-done(((f32[32,1,2816]{2,1,0:T(1,128)}), f32[32,1,2816]{2,1,0:T(1,128)S(1)}, u32[]{:S(2)}, u32[]{:S(2)}) %all-to-all-start.1) | async-done | bytes 360480 | tf_op jit(solution)/shard_map/all_to_all | solution.py:248
  652.3 5.4 reshape.894
  657.7 2.1 copy.239
  659.9 4.8 copy.199
  664.7 4.7 all_to_all.55
  669.3 5.9 reshape.797
  675.3 3.5 slice.293
  679.1 3.2 slice_add_fusion
  682.4 21.2 %scatter-add.9 = f32[32,8,2,8,16]{1,0,4,3,2:T(8,128)} dynamic-update-slice(f32[32,8,2,8,16]{1,0,4,3,2:T(8,128)} %bitcast.446, f32[32,3,2,8,16]{1,0,4,3,2:T(8,128)} %slice_add_fusion, s32[]{:T(128)} %constant.152.clone.1, s32[]{:T(128)} %constant.152.clone.1, s32[]{:T(128)} %constant.152.clone.1, s32[]{:T(128)} %constant.152.clone.1, s32[]{:T(128)} %constant.152.clone.1) | dynamic-update-slice | bytes 196612 | tf_op jit(solution)/shard_map/scatter-add | solution.py:162
  703.5 4.3 copy.200
  719.4 2.5 copy.202
  722.2 2.3 copy.203
  724.5 2.1 fusion.28
  727.6 16.8 %all_to_all.66 = f32[32,1,2816]{2,1,0:T(1,128)S(1)} all-to-all(f32[32,1,2816]{2,1,0:T(1,128)S(1)} %reshape.895), channel_id=1, replica_groups=mesh['brick'=32,'slab'=16] {'brick'}, dimensions={0} | all-to-all | bytes 720896 | tf_op jit(solution)/shard_map/all_to_all | solution.py:256
  746.9 4.7 copy.229
  751.6 4.2 fusion.219
  755.8 3.2 copy.210
  759.0 3.6 fusion.29
  762.5 3.6 fusion.31
  766.1 2.3 copy.208
  768.4 3.8 fusion.50
  772.3 3.8 fusion.44
  778.0 3.1 slice.255
  781.1 4.6 fusion.27
  785.7 6.0 copy.215
  791.8 4.8 reshape.897
  796.5 4.4 all-to-all-start.3
  801.1 15.9 %all-to-all-done.3 = f32[16,1,6688]{2,1,0:T(1,128)S(1)} async-done(((f32[16,1,6688]{2,1,0:T(1,128)}), f32[16,1,6688]{2,1,0:T(1,128)S(1)}, u32[]{:S(2)}, u32[]{:S(2)}) %all-to-all-start.3) | async-done | bytes 428064 | tf_op jit(solution)/shard_map/all_to_all | solution.py:258
  817.0 2.5 reduce.24
  819.5 3.2 reshape.898
  822.8 5.0 copy.230
  827.8 3.2 fusion.220
  831.0 2.4 copy.217
  834.2 2.0 fusion.63
  (1021 shorter events, 497.7 us)
Async XLA Ops:
  0.6 27.1 %copy-start.5 = (f32[25,50]{1,0:T(8,128)S(1)}, f32[25,50]{1,0:T(8,128)}, u32[]{:S(2)}) copy-start(f32[25,50]{1,0:T(8,128)} %param.35) | copy-start | bytes 15004
  0.6 27.1 %copy-start.8 = (f32[240]{0:T(256)S(1)}, f32[240]{0:T(256)}, u32[]{:S(2)}) copy-start(f32[240]{0:T(256)} %param.39) | copy-start | bytes 2884
  0.7 27.1 %copy-start.9 = (f32[240]{0:T(256)S(1)}, f32[240]{0:T(256)}, u32[]{:S(2)}) copy-start(f32[240]{0:T(256)} %param.42) | copy-start | bytes 2884
  3.6 23.8 %collective-permute-start.1 = (f32[4,96]{0,1:T(8,128)S(1)}, f32[4,96]{0,1:T(8,128)S(1)}, u32[]{:S(2)}, u32[]{:S(2)}) collective-permute-start(f32[4,96]{0,1:T(8,128)S(1)} %get-tuple-element.233), channel_id=1, source_target_pairs={{16,0},{32,16},{48,32},{64,48},{80,64},{96,80},{112,96},{128,112},... | collective-permute-start | bytes 4616 | tf_op jit(solution)/shard_map/ppermute | solution.py:24
  12.4 15.0 %collective-permute-start = (f32[4,96]{0,1:T(8,128)S(1)}, f32[4,96]{0,1:T(8,128)S(1)}, u32[]{:S(2)}, u32[]{:S(2)}) collective-permute-start(f32[4,96]{0,1:T(8,128)S(1)} %get-tuple-element.232), channel_id=1, source_target_pairs={{0,16},{16,32},{32,48},{48,64},{64,80},{80,96},{96,112},{112,128},... | collective-permute-start | bytes 4616 | tf_op jit(solution)/shard_map/ppermute | solution.py:22
  22.3 4.1 copy-start.6
  27.8 487.5 %copy-start.12 = (f32[1,192]{1,0:T(1,128)S(1)}, f32[1,192]{1,0:T(1,128)}, u32[]{:S(2)}) copy-start(f32[1,192]{1,0:T(1,128)} %multiply_add_fusion.1) | copy-start | bytes 2308
  27.8 13.4 %copy-start.14 = (s32[3,64]{1,0:T(4,128)}, s32[3,64]{1,0:T(4,128)S(1)}, u32[]{:S(2)}) copy-start(s32[3,64]{1,0:T(4,128)S(1)} %get-tuple-element.475) | copy-start | bytes 2308 | tf_op jit(solution)/shard_map/while
  179.9 1.6 copy-start.1
  181.5 1.6 copy-start.2
  183.1 5.0 copy-start.3
  183.1 6.9 copy-start.15
  190.0 13.4 %copy-start.14 = (s32[3,64]{1,0:T(4,128)}, s32[3,64]{1,0:T(4,128)S(1)}, u32[]{:S(2)}) copy-start(s32[3,64]{1,0:T(4,128)S(1)} %get-tuple-element.475) | copy-start | bytes 2308 | tf_op jit(solution)/shard_map/while
  342.1 1.6 copy-start.1
  343.7 1.6 copy-start.2
  345.2 5.0 copy-start.3
  345.3 6.9 copy-start.15
  352.2 13.4 %copy-start.14 = (s32[3,64]{1,0:T(4,128)}, s32[3,64]{1,0:T(4,128)S(1)}, u32[]{:S(2)}) copy-start(s32[3,64]{1,0:T(4,128)S(1)} %get-tuple-element.475) | copy-start | bytes 2308 | tf_op jit(solution)/shard_map/while
  504.3 1.6 copy-start.1
  505.8 1.6 copy-start.2
  507.4 5.0 copy-start.3
  507.4 6.9 copy-start.15
  527.7 24.5 %all-to-all-start = ((f32[16,1,6688]{2,1,0:T(1,128)}), f32[16,1,6688]{2,1,0:T(1,128)S(1)}, u32[]{:S(2)}, u32[]{:S(2)}) async-start(f32[16,1,6688]{2,1,0:T(1,128)} %reshape.891), calls=%async_computation | async-start | bytes 868352 | tf_op jit(solution)/shard_map/all_to_all | solution.py:246
  625.9 24.9 %all-to-all-start.1 = ((f32[32,1,2816]{2,1,0:T(1,128)}), f32[32,1,2816]{2,1,0:T(1,128)S(1)}, u32[]{:S(2)}, u32[]{:S(2)}) async-start(f32[32,1,2816]{2,1,0:T(1,128)} %reshape.893), calls=%async_computation.1 | async-start | bytes 720896 | tf_op jit(solution)/shard_map/all_to_all | solution.py:248
  675.3 3.5 copy-start
  791.8 9.2 %copy-start.11 = (f32[3,64]{1,0:T(4,128)S(1)}, f32[3,64]{1,0:T(4,128)}, u32[]{:S(2)}) copy-start(f32[3,64]{1,0:T(4,128)} %get-tuple-element.110) | copy-start | bytes 2308
  791.8 9.3 %copy-start.13 = (f32[3,64]{1,0:T(4,128)S(1)}, f32[3,64]{1,0:T(4,128)}, u32[]{:S(2)}) copy-start(f32[3,64]{1,0:T(4,128)} %get-tuple-element.109) | copy-start | bytes 2308
  796.5 20.5 %all-to-all-start.3 = ((f32[16,1,6688]{2,1,0:T(1,128)}), f32[16,1,6688]{2,1,0:T(1,128)S(1)}, u32[]{:S(2)}, u32[]{:S(2)}) async-start(f32[16,1,6688]{2,1,0:T(1,128)} %reshape.897), calls=%async_computation.3 | async-start | bytes 868352 | tf_op jit(solution)/shard_map/all_to_all | solution.py:258
  836.3 2.2 copy-start.16
  837.6 2.2 copy-start.4
  837.6 2.2 copy-start.7
  837.7 3.7 copy-start.10
where the time goes:
time: 859 us; the launch traced here: 844 us
  local copies, waits for them, and re-layouts  626 us (73%)
  matrix products  76.7 us (9%)
  waiting for transfers between devices  41.7 us (5%)
  other arithmetic  40.5 us (5%)
  starting transfers between devices  38.3 us (4%)
  blocking collectives  16.8 us (2%)
    gather x768, local copies, waits for them, and re-layouts  384 us
    scatter-add x3, local copies, waits for them, and re-layouts, fold_windows(): main_part = main_part.at[:, :3].add(carried)  52.6 us
    unnamed x39, local copies, waits for them, and re-layouts  42.1 us
    gather x6, local copies, waits for them, and re-layouts, one_block(): gathered = extended[:, rows_block]  34.4 us
    dot_general x12, matrix products, along(): jnp.tensordot(values, table, axes=([axis_index], [0]), precision=HIGH)  26.2 us
  transfers between devices with their start and end apart: 5, of which 3 were waited for; matrix products, arithmetic and copies ran while one was open for 2% of the time, Pallas kernels for 0%

commit v1 on v0

v1 whole, which is shorter than its diff:
```python
import math

import jax
import jax.numpy as jnp
import numpy as np
from jax import lax
from jax.experimental import pallas as pl
from jax.experimental.pallas import tpu as pltpu
from jax.sharding import PartitionSpec as P

NG = 256
A = 192
NB = 32
NS = 16
CX = 8
CY = 16
WX = 11
WY = 24
MIB = 1024 * 1024
F32 = jnp.float32
BF16 = jnp.bfloat16
HIGH = lax.Precision.HIGH
HIGHEST = lax.Precision.HIGHEST
MESH = pl.DeviceIdType.MESH

NN = (((1,), (0,)), ((), ()))
NT = (((1,), (1,)), ((), ()))


def split(table):
    table = np.asarray(table, np.float64)
    high = np.asarray(table, np.float32).astype(jnp.bfloat16)
    low = (table - high.astype(np.float64)).astype(np.float32).astype(jnp.bfloat16)
    return high, low


def real_basis():
    n = np.arange(NG)[:, None]
    j = np.arange(NG)[None, :]
    phase = 2.0 * np.pi * ((n * j) % NG) / NG
    basis = np.where(j <= NG // 2, np.cos(phase), np.sin(phase)) * math.sqrt(2.0 / NG)
    basis[:, 0] = 1.0 / 16.0
    basis[:, NG // 2] = np.where(np.arange(NG) % 2 == 0, 1.0, -1.0) / 16.0
    return basis


def transform_tables():
    basis = real_basis()
    slab, offset = np.divmod(np.arange(NS * WY), WY)
    window = basis[(slab * CY + offset) % NG] * (offset < CY + 3)[:, None]
    b = np.arange(NB)
    angle = 2.0 * np.pi * np.outer(b, b) / NB
    eye8 = np.eye(8)
    cos_b = np.kron(np.cos(angle), eye8)
    sin_b = np.kron(np.sin(angle), eye8)
    left = np.concatenate([cos_b, sin_b], axis=0)
    left_back = np.concatenate([cos_b, -sin_b], axis=1)
    xw = np.arange(16)
    live = (xw < WX)[:, None]
    small = 2.0 * np.pi * np.outer(xw, np.arange(8)) / 8
    eye16 = np.eye(16)
    cos_m = np.kron(np.cos(small) * live, eye16)
    sin_m = np.kron(np.sin(small) * live, eye16)
    right = np.block([[cos_m, -sin_m], [sin_m, cos_m]])
    right_back = np.block([[cos_m.T, sin_m.T], [-sin_m.T, cos_m.T]])
    kb = np.repeat(b, 8)[:, None]
    lane_x = np.repeat(xw, 16)[None, :]
    twist = 2.0 * np.pi * kb * lane_x / NG
    return {
        "y": split(window.T),
        "y_back": split(window),
        "left": split(left),
        "left_back": split(left_back),
        "right": split(right),
        "right_back": split(right_back),
        "twist": (np.cos(twist).astype(np.float32), np.sin(twist).astype(np.float32)),
        "z": split(basis),
        "z_back": split(basis.T),
    }


def second_rows():
    rows = list(range(24)) + list(range(25, 49)) + [24, 49, 24, 49]
    return rows


def third_rows():
    second = second_rows()
    return [f for f in second[:48]] + [50 + f for f in second[:48]] + [24, 49, 74, 99]


def one_hot(rows, height, width):
    table = np.zeros((height, width), np.float32)
    for row, feature in enumerate(rows):
        table[row, feature] = 1.0
    return table


def embedding_tables():
    first = one_hot(list(range(25)) + [24, 24, 24], 32, 25)
    second = one_hot(second_rows(), 64, 50)
    third = one_hot(third_rows(), 112, 100)
    columns_first = np.tile(np.eye(25, 32, dtype=np.float32), (1, 3))
    placed = np.zeros((50, 64), np.float32)
    for row, feature in enumerate(second_rows()[:50]):
        placed[feature, row] = 1.0
    columns_second = np.tile(placed, (1, 3))
    place = np.zeros(104, np.int32)
    for row, feature in enumerate(third_rows()):
        place[feature] = row
    lanes = np.arange(13 * 128) // 16
    spread = place[lanes].reshape(13, 128).astype(np.int32)
    spread = np.concatenate([spread, np.zeros((3, 128), np.int32)])
    return first, second, third, columns_first, columns_second, spread


def halves(values):
    high = values.astype(BF16)
    low = (values - high.astype(F32)).astype(BF16)
    return high, low


def dot(a, b, dims=NN):
    return lax.dot_general(a, b, dims, preferred_element_type=F32)


def dot3(a, b, dims=NN):
    return dot(a[0], b[0], dims) + (dot(a[0], b[1], dims) + dot(a[1], b[0], dims))


def lanes_iota(shape):
    return lax.broadcasted_iota(jnp.int32, shape, 1)


def rows_iota(shape):
    return lax.broadcasted_iota(jnp.int32, shape, 0)


def pick(row, index):
    table = jnp.broadcast_to(row, index.shape)
    return jnp.take_along_axis(table, index, axis=1, mode="promise_in_bounds")


def spline_rows(u):
    cubed = u * u * u
    square = u * u
    rest = 1.0 - u
    return (
        rest * rest * rest / 6.0,
        (3.0 * cubed - 6.0 * square + 4.0) / 6.0,
        (-3.0 * cubed + 3.0 * square + 3.0 * u + 1.0) / 6.0,
        cubed / 6.0,
    )


def place_rows(start, weights, height, wrap):
    offset = rows_iota((height, A)) - start
    if wrap:
        offset = offset & (wrap - 1)
    result = jnp.zeros((height, A), F32)
    for step in range(4):
        result = jnp.where(offset == step, weights[step], result)
    return result


def spreads(cx_ref, cy_ref, cz_ref, frac_ref):
    wx = place_rows(cx_ref[...], spline_rows(frac_ref[0]), 16, 0)
    wy = place_rows(cy_ref[...], spline_rows(frac_ref[1]), WY, 0)
    wz = place_rows(cz_ref[...], spline_rows(frac_ref[2]), NG, NG)
    wxy = jnp.concatenate([wx[x : x + 1] * wy for x in range(WX)], axis=0)
    return wxy, wz


def atoms_kernel(
    own_ref, low_ref, upp_ref, count_ref, neigh_ref,
    cx_ref, cy_ref, cz_ref, frac_ref,
    first_ref, second_ref, third_ref,
    e_in_ref, e_hid_ref, e_out_ref, w_in_ref, w_hid_ref, w_out_ref, base_ref,
    p1_ref, p2_ref, p3_ref, c1_ref, c2_ref, spread_ref, zh_ref, zl_ref,
    scal_ref, send_ref,
    env_ref, moment_ref, desc_h_ref, desc_l_ref, w2_ref, w3_ref,
):
    f1 = lax.dot_general(p1_ref[...], first_ref[...], NT, precision=HIGHEST)
    oxygen, hydrogen = f1[:, 0:1], f1[:, 1:2]
    w2 = lax.dot_general(p2_ref[...], second_ref[...], NT, precision=HIGHEST)
    w2 = lax.dot_general(w2, c1_ref[...], NN, precision=HIGHEST)
    high, low = halves(w2)
    slot = lanes_iota((64, 96)) // 32
    w2_ref[...] = jnp.where(slot == 1, low.astype(F32), high.astype(F32)).astype(BF16)
    w3 = lax.dot_general(p3_ref[...], third_ref[...], NT, precision=HIGHEST)
    w3 = lax.dot_general(w3, c2_ref[...], NN, precision=HIGHEST)
    high, low = halves(w3)
    slot = lanes_iota((112, 192)) // 64
    w3_ref[...] = jnp.where(slot == 1, low.astype(F32), high.astype(F32)).astype(BF16)

    n = jnp.concatenate([neigh_ref[0, 0:96, :], neigh_ref[0, 96:192, :]], axis=1)
    low_index = pick_index = (n - 96) & 127
    lower_index = n & 127
    upper_index = (n - 288) & 127
    lane = lanes_iota((96, 128))
    centre = rows_iota((96, 128)) + jnp.where(lane >= 64, 96, 0)
    centre_index = centre & 127
    ghosts_low = jnp.broadcast_to(low_ref[5:6, 0:128], (8, 128)).astype(jnp.int32)
    ghosts_upp = jnp.broadcast_to(upp_ref[4:5, 0:128], (8, 128)).astype(jnp.int32)

    def ghost_rows(ref, index):
        near = jnp.take_along_axis(ref[:, 0:128], index & 127, axis=1, mode="promise_in_bounds")
        far = jnp.take_along_axis(ref[:, 128:256], index & 127, axis=1, mode="promise_in_bounds")
        return jnp.where(index < 128, near, far)

    lower = ghost_rows(low_ref, ghosts_low)
    upper = ghost_rows(upp_ref, ghosts_upp)
    gathered = []
    for c in range(4):
        value = pick(own_ref[c : c + 1, 0:128], pick_index)
        value = jnp.where(n < 224, value, pick(own_ref[c : c + 1, 128:256], pick_index))
        value = jnp.where(n < 96, pick(lower[c : c + 1], lower_index), value)
        value = jnp.where(n >= 288, pick(upper[c : c + 1], upper_index), value)
        gathered.append(value)
    offsets = []
    for c in range(3):
        here = jnp.where(
            centre < 128,
            pick(own_ref[c : c + 1, 0:128], centre_index),
            pick(own_ref[c : c + 1, 128:256], centre_index),
        )
        offsets.append(gathered[c] - here)
    total = jnp.where(
        centre < 128,
        pick(count_ref[0:1, 0:128], centre_index),
        pick(count_ref[0:1, 128:256], centre_index),
    )
    squared = offsets[0] * offsets[0] + offsets[1] * offsets[1] + offsets[2] * offsets[2]
    smooth = jnp.where((lane & 63).astype(F32) < total, 1.0 / (1.0 + squared), 0.0)
    env_ref[0] = smooth
    for c in range(3):
        env_ref[c + 1] = smooth * offsets[c]
    env_ref[4] = gathered[3]

    oxygen_wide = jnp.broadcast_to(oxygen, (32, 128))
    hydrogen_wide = jnp.broadcast_to(hydrogen, (32, 128))
    row8 = rows_iota((8, 128))
    left8 = lanes_iota((8, 128)) < 64

    def chunk(step, carry):
        at = pl.multiple_of(step * 8, 8)
        first = []
        for r in range(8):
            sm = env_ref[0, pl.ds(at + r, 1), :]
            kind = env_ref[4, pl.ds(at + r, 1), :]
            mixing = jnp.where(kind > 0.5, hydrogen_wide, oxygen_wide)
            first.append(jnp.tanh(sm * mixing))
        first = jnp.concatenate(first, axis=1)
        high, low = halves(first)
        second = dot(w2_ref[...], jnp.concatenate([high, high, low], axis=0))
        second = jnp.tanh(second[:56]) + jnp.concatenate([first[:24], first], axis=0)
        padded = jnp.concatenate([second, jnp.zeros((8, 1024), F32)], axis=0)
        high, low = halves(padded)
        third = dot(w3_ref[...], jnp.concatenate([high, high, low], axis=0))
        third = jnp.tanh(third[:104]) + jnp.concatenate([second[:48], second], axis=0)
        third = jnp.concatenate([third, jnp.zeros((8, 1024), F32)], axis=0)
        third = halves(third)
        rows = []
        for c in range(4):
            value = env_ref[c, pl.ds(at, 8), :] * (1.0 / 64.0)
            for half in range(2):
                side = left8 if half == 0 else jnp.logical_not(left8)
                kept = jnp.where(side, value, 0.0)
                rows.append(
                    jnp.concatenate([jnp.where(row8 == r, kept, 0.0) for r in range(8)], axis=1)
                )
        rows = halves(jnp.concatenate(rows, axis=0))
        both = dot(jnp.concatenate(rows, axis=0), third[0], NT)
        moments = both[:64] + both[64:] + dot(rows[0], third[1], NT)
        for c in range(4):
            for half in range(2):
                k = (c * 2 + half) * 8
                moment_ref[c, pl.ds(at + half * 96, 8), 0:112] = moments[k : k + 8]
        return carry

    lax.fori_loop(0, 12, chunk, 0)

    lane_a = lanes_iota((A, 128))
    moments = [jnp.where(lane_a < 104, moment_ref[c], 0.0) for c in range(4)]
    factors = [
        jnp.take_along_axis(m, lane_a & 15, axis=1, mode="promise_in_bounds") for m in moments
    ]
    for j in range(13):
        index = jnp.broadcast_to(spread_ref[j : j + 1, :], (A, 128))
        value = None
        for c in range(4):
            term = jnp.take_along_axis(moments[c], index, axis=1, mode="promise_in_bounds")
            term = term * factors[c]
            value = term if value is None else value + term
        high, low = halves(value)
        desc_h_ref[:, j * 128 : (j + 1) * 128] = high
        desc_l_ref[:, j * 128 : (j + 1) * 128] = low

    def network(in_ref, hid_ref, out_ref):
        weight = halves(in_ref[...])
        hidden = jnp.tanh(dot3((desc_h_ref[:, 0:1600], desc_l_ref[:, 0:1600]), weight))
        for layer in range(2):
            hidden = jnp.tanh(dot3(halves(hidden), halves(hid_ref[layer]))) + hidden
        row = jnp.broadcast_to(out_ref[...], (16, 240))
        return dot3(halves(row), halves(hidden), NT)[0:1]

    energy = network(e_in_ref, e_hid_ref, e_out_ref)
    shift = network(w_in_ref, w_hid_ref, w_out_ref)
    charge = jnp.where(own_ref[3:4, 0:A] > 0.5, base_ref[1], base_ref[0]) + shift
    scal_ref[...] = jnp.concatenate([energy, charge, jnp.zeros((6, A), F32)], axis=0)

    wxy, wz = spreads(cx_ref, cy_ref, cz_ref, frac_ref)
    grid = dot3(halves(wxy), halves(wz * charge), NT)
    spectrum = dot3(halves(grid), (zh_ref[...], zl_ref[...]))
    chunk_lane = lanes_iota((WY, 128)) // 16
    for s in range(NS):
        tile, chunk_from = divmod(s, 8)
        for half in range(2):
            out = jnp.zeros((WY, 128), F32)
            for x in range(8 * half, min(8 * half + 8, WX)):
                source = spectrum[x * WY : (x + 1) * WY, tile * 128 : (tile + 1) * 128]
                shift_by = 16 * (x % 8 - chunk_from) % 128
                if shift_by:
                    source = pltpu.roll(source, shift_by, 1)
                out = jnp.where(chunk_lane == x % 8, source, out)
            send_ref[s, :, half * 128 : (half + 1) * 128] = out


def solve_kernel(
    send_ref, yh_ref, yl_ref, lh_ref, ll_ref, rh_ref, rl_ref, tc_ref, ts_ref,
    rbh_ref, rbl_ref, lbh_ref, lbl_ref, ybh_ref, ybl_ref,
    out_ref,
    in1, out2, in2, out3, in3, out4,
    send1, recv1, send2, recv2, send3, recv3, send4, recv4,
):
    b = lax.axis_index("brick")
    s = lax.axis_index("slab")

    barrier = pltpu.get_barrier_semaphore()

    def greet_slab(i, carry):
        pl.semaphore_signal(barrier, inc=1, device_id=(b, lax.rem(s + i, NS)), device_id_type=MESH)
        return carry

    def greet_brick(i, carry):
        pl.semaphore_signal(barrier, inc=1, device_id=(lax.rem(b + i, NB), s), device_id_type=MESH)
        return carry

    lax.fori_loop(1, NS, greet_slab, 0)
    lax.fori_loop(1, NB, greet_brick, 0)
    pl.semaphore_wait(barrier, NS + NB - 2)

    def over_slab(source, target, send_sem, recv_sem):
        def copy(i):
            to = lax.rem(s + i, NS)
            return pltpu.make_async_remote_copy(
                src_ref=source.at[to],
                dst_ref=target.at[s],
                send_sem=send_sem.at[to],
                recv_sem=recv_sem.at[s],
                device_id=(b, to),
                device_id_type=MESH,
            )

        def arrival(i):
            frm = lax.rem(s + i, NS)
            return pltpu.make_async_remote_copy(
                src_ref=source.at[frm],
                dst_ref=target.at[frm],
                send_sem=send_sem.at[frm],
                recv_sem=recv_sem.at[frm],
                device_id=(b, frm),
                device_id_type=MESH,
            )

        def start(i, carry):
            copy(i).start()
            return carry

        def wait(i, carry):
            arrival(i).wait_recv()
            return carry

        def drain(i, carry):
            copy(i).wait_send()
            return carry

        lax.fori_loop(1, NS, start, 0)
        target[s] = source[s]
        lax.fori_loop(1, NS, wait, 0)
        return lambda: lax.fori_loop(1, NS, drain, 0)

    def over_brick(source, target, send_sem, recv_sem):
        def copy(i):
            to = lax.rem(b + i, NB)
            return pltpu.make_async_remote_copy(
                src_ref=source.at[to],
                dst_ref=target.at[b],
                send_sem=send_sem.at[to],
                recv_sem=recv_sem.at[b],
                device_id=(to, s),
                device_id_type=MESH,
            )

        def arrival(i):
            frm = lax.rem(b + i, NB)
            return pltpu.make_async_remote_copy(
                src_ref=source.at[frm],
                dst_ref=target.at[frm],
                send_sem=send_sem.at[frm],
                recv_sem=recv_sem.at[frm],
                device_id=(frm, s),
                device_id_type=MESH,
            )

        def start(i, carry):
            copy(i).start()
            return carry

        def wait(i, carry):
            arrival(i).wait_recv()
            return carry

        def drain(i, carry):
            copy(i).wait_send()
            return carry

        lax.fori_loop(1, NB, start, 0)
        target[b] = source[b]
        lax.fori_loop(1, NB, wait, 0)
        return lambda: lax.fori_loop(1, NB, drain, 0)

    drain1 = over_slab(send_ref, in1, send1, recv1)
    data = halves(in1[...].reshape(NS * WY, NG))
    out2[...] = dot3((yh_ref[...], yl_ref[...]), data).reshape(NB, 8, NG)
    drain2 = over_brick(out2, in2, send2, recv2)

    row = rows_iota((256, 128))
    lane = lanes_iota((256, 128))

    def kappa(index):
        folded = jnp.minimum(index, NG - index)
        return folded.astype(F32) * (2.0 * math.pi / NG)

    kx = kappa(row // 8 + 32 * (lane // 16))
    ky = kappa(b * 8 + row % 8)
    kz = kappa(s * 16 + lane % 16)
    squared = kx * kx + ky * ky + kz * kz
    root = jnp.where(squared == 0.0, 1.0, 0.0)
    green = (1.0 - root) * jnp.exp(-0.5 * squared) / (squared + root) * (1.0 / NG)
    green = jnp.concatenate([green, green], axis=1)

    data = halves(in2[...].reshape(256, NG))
    both = dot3((lh_ref[...], ll_ref[...]), data)
    uc, us = both[:256], both[256:]
    tc, ts = tc_ref[...], ts_ref[...]
    turned = jnp.concatenate([uc * tc - us * ts, -(uc * ts + us * tc)], axis=1)
    modes = dot3(halves(turned), (rh_ref[...], rl_ref[...])) * green
    back = dot3(halves(modes), (rbh_ref[...], rbl_ref[...]))
    vr, vi = back[:, :256], back[:, 256:]
    turned = jnp.concatenate([vr * tc - vi * ts, vr * ts + vi * tc], axis=0)
    out3[...] = dot3((lbh_ref[...], lbl_ref[...]), halves(turned)).reshape(NB, 8, NG)
    drain3 = over_brick(out3, in3, send3, recv3)
    data = halves(in3[...].reshape(256, NG))
    out4[...] = dot3((ybh_ref[...], ybl_ref[...]), data).reshape(NS, WY, NG)
    drain4 = over_slab(out4, out_ref, send4, recv4)
    drain1()
    drain2()
    drain3()
    drain4()


def sample_kernel(
    in_ref, cx_ref, cy_ref, cz_ref, frac_ref, scal_ref, zh_ref, zl_ref, energy_ref, pot_ref, modes_ref
):
    chunk_lane = lanes_iota((WY, 128)) // 16
    for x in range(WX):
        half, chunk_from = divmod(x, 8)
        for tile in range(2):
            out = jnp.zeros((WY, 128), F32)
            for c in range(8):
                source = in_ref[8 * tile + c, :, half * 128 : (half + 1) * 128]
                shift_by = 16 * (c - chunk_from) % 128
                if shift_by:
                    source = pltpu.roll(source, shift_by, 1)
                out = jnp.where(chunk_lane == c, source, out)
            modes_ref[x * WY : (x + 1) * WY, tile * 128 : (tile + 1) * 128] = out
    potential = dot3(halves(modes_ref[...]), (zh_ref[...], zl_ref[...]))
    for x in range(CX):
        pot_ref[x] = potential[x * WY : x * WY + CY]
    wxy, wz = spreads(cx_ref, cy_ref, cz_ref, frac_ref)
    sampled = dot3(halves(potential), halves(wz))
    at = jnp.sum(sampled * wxy, axis=0, keepdims=True)
    energy_ref[...] = scal_ref[0:1, :] + 0.5 * scal_ref[1:2, :] * at


VMEM = pl.BlockSpec(memory_space=pltpu.VMEM)
SMEM = pl.BlockSpec(memory_space=pltpu.SMEM)


def per_device(
    positions, types, neighbours, neighbour_count, send_index, cell_x, cell_y, cell_z, spline_fraction,
    embed_first, embed_second, embed_third, energy_in, energy_hidden, energy_out,
    wannier_in, wannier_hidden, wannier_out, charge_base,
):
    tables = transform_tables()
    embedding = embedding_tables()

    def wide(rows):
        return jnp.pad(rows, ((0, 0), (0, 256 - rows.shape[1])))

    own = jnp.concatenate(
        [
            wide(positions[:, 0]),
            wide(types.astype(F32)),
            wide(send_index[:, :96].astype(F32)),
            wide(send_index[:, 96:].astype(F32)),
            jnp.zeros((2, 256), F32),
        ],
        axis=0,
    )
    lower = lax.ppermute(own, "brick", [(i, (i + 1) % NB) for i in range(NB)])
    upper = lax.ppermute(own, "brick", [((i + 1) % NB, i) for i in range(NB)])
    count = wide(neighbour_count.astype(F32))

    scalars, send = pl.pallas_call(
        atoms_kernel,
        out_shape=(
            jax.ShapeDtypeStruct((8, A), F32),
            jax.ShapeDtypeStruct((NS, WY, NG), F32),
        ),
        in_specs=[VMEM] * 18 + [SMEM] + [VMEM] * 8,
        out_specs=(VMEM, VMEM),
        scratch_shapes=[
            pltpu.VMEM((5, 96, 128), F32),
            pltpu.VMEM((4, A, 128), F32),
            pltpu.VMEM((A, 1664), BF16),
            pltpu.VMEM((A, 1664), BF16),
            pltpu.VMEM((64, 96), BF16),
            pltpu.VMEM((112, 192), BF16),
        ],
        compiler_params=pltpu.CompilerParams(vmem_limit_bytes=48 * MIB),
        name="atoms",
    )(
        own, lower, upper, count, neighbours,
        cell_x, cell_y, cell_z, spline_fraction,
        embed_first, embed_second, embed_third,
        energy_in, energy_hidden, energy_out.reshape(1, -1),
        wannier_in, wannier_hidden, wannier_out.reshape(1, -1), charge_base,
        *embedding, *tables["z"],
    )

    received = pl.pallas_call(
        solve_kernel,
        out_shape=jax.ShapeDtypeStruct((NS, WY, NG), F32),
        in_specs=[VMEM] * 15,
        out_specs=VMEM,
        scratch_shapes=[
            pltpu.VMEM((NS, WY, NG), F32),
            pltpu.VMEM((NB, 8, NG), F32),
            pltpu.VMEM((NB, 8, NG), F32),
            pltpu.VMEM((NB, 8, NG), F32),
            pltpu.VMEM((NB, 8, NG), F32),
            pltpu.VMEM((NS, WY, NG), F32),
            pltpu.SemaphoreType.DMA((NS,)),
            pltpu.SemaphoreType.DMA((NS,)),
            pltpu.SemaphoreType.DMA((NB,)),
            pltpu.SemaphoreType.DMA((NB,)),
            pltpu.SemaphoreType.DMA((NB,)),
            pltpu.SemaphoreType.DMA((NB,)),
            pltpu.SemaphoreType.DMA((NS,)),
            pltpu.SemaphoreType.DMA((NS,)),
        ],
        compiler_params=pltpu.CompilerParams(
            collective_id=1, has_side_effects=True, vmem_limit_bytes=40 * MIB
        ),
        name="solve",
    )(
        send, *tables["y"], *tables["left"], *tables["right"], *tables["twist"],
        *tables["right_back"], *tables["left_back"], *tables["y_back"],
    )

    energy, potential = pl.pallas_call(
        sample_kernel,
        out_shape=(
            jax.ShapeDtypeStruct((1, A), F32),
            jax.ShapeDtypeStruct((CX, CY, NG), F32),
        ),
        in_specs=[VMEM] * 8,
        out_specs=(VMEM, VMEM),
        scratch_shapes=[pltpu.VMEM((WX * WY, NG), F32)],
        compiler_params=pltpu.CompilerParams(vmem_limit_bytes=40 * MIB),
        name="sample",
    )(received, cell_x, cell_y, cell_z, spline_fraction, scalars, *tables["z_back"])
    return energy, potential


def solution(mesh):
    row = P("slab", "brick")
    three = P(None, "slab", "brick")
    placed = (three, row, P("slab", "brick", None), row, row, row, row, row, three) + (P(),) * 10
    return jax.shard_map(
        per_device,
        mesh=mesh,
        in_specs=placed,
        out_specs=(row, P("brick", "slab", None)),
        check_vma=False,
    )
```

time: 859 us -> 110 us (0.13); the launches traced: 844 us -> 109 us
  local copies, waits for them, and re-layouts: 626 us -> 18.8 us
  matrix products: 76.7 us -> 0 us
  Pallas kernels: 0 us -> 76.4 us
  waiting for transfers between devices: 41.7 us -> 0.01 us
  other arithmetic: 40.5 us -> 2.17 us
  starting transfers between devices: 38.3 us -> 10.7 us
  blocking collectives: 16.8 us -> 0 us
    gather x775 -> x0, local copies, waits for them, and re-layouts: 419 us -> none
    pallas_call x0 -> x3, Pallas kernels: none -> 76.4 us  [the longest x1 57.8 us: per_device(): pl.pallas_call(solve_kernel, out_shape=jax.ShapeDtypeStruct((NS, WY, NG),...]
    dot_general x50 -> x0, matrix products: 66.5 us -> none  [the longest x12 26.2 us: along(): jnp.tensordot(values, table, axes=([axis_index], [0]), precision=HIGH)]
    scatter-add x3 -> x0, local copies, waits for them, and re-layouts: 52.6 us -> none  [fold_windows(): main_part = main_part.at[:, :3].add(carried)]
    all_to_all x3 -> x0, waiting for transfers between devices: 41.7 us -> none  [the longest x1 15.9 us: per_device(): lax.all_to_all(moved, 'slab', split_axis=2, concat_axis=3, tiled=True)]
    slice x22 -> x0, local copies, waits for them, and re-layouts: 32.7 us -> none  [the longest x4 7.32 us: fold_windows(): carried = jnp.roll(windows[:, block:], 1, axis=0)]
    all_to_all x8 -> x0, local copies, waits for them, and re-layouts: 27.9 us -> none  [the longest x3 11.6 us: per_device(): lax.all_to_all(moved, 'brick', split_axis=2, concat_axis=1, tiled=True)]
    all_to_all x3 -> x0, starting transfers between devices: 27.6 us -> none  [the longest x1 11.7 us: per_device(): lax.all_to_all(moved, 'brick', split_axis=2, concat_axis=1, tiled=True)]
  transfers between devices with their start and end apart: 5 -> 2, of which waited for: 3 -> 0; matrix products, arithmetic and copies ran while one was open for 2% -> 5% of each run, Pallas kernels for 0% -> 0%
where the time goes in v1:
time: 110 us; the launch traced here: 109 us
  Pallas kernels  76.4 us (69%)
  local copies, waits for them, and re-layouts  18.8 us (17%)
  starting transfers between devices  10.7 us (10%)
  other arithmetic  2.17 us (2%)
    pallas_call x1, Pallas kernels, per_device(): pl.pallas_call(solve_kernel, out_shape=jax.ShapeDtypeStruct((NS, WY, NG),...  57.8 us
    unnamed x78, local copies, waits for them, and re-layouts  18.2 us
    pallas_call x1, Pallas kernels, per_device(): pl.pallas_call(atoms_kernel, out_shape=(jax.ShapeDtypeStruct((8, A), F32)...  16.9 us
    ppermute x1, starting transfers between devices, per_device(): upper = lax.ppermute(own, 'brick', [((i + 1) % NB, i) for i in range(NB)])  8.79 us
  transfers between devices with their start and end apart: 2, of which 0 were waited for; matrix products, arithmetic and copies ran while one was open for 5% of the time, Pallas kernels for 0%

profile of v1, /device:TPU:1, one launch (start us, length us, event | category | flops | bytes accessed | tf_op | source)
XLA Modules:
  0.0 109.1 jit_solution(17944965607438936017)
XLA Ops:
  0.6 0.7 convert_element_type.20
  1.3 0.8 slice_convert_fusion
  2.1 0.7 copy.50
  2.9 8.8 %collective-permute-start.1 = (f32[8,256]{1,0:T(8,128)S(1)}, f32[8,256]{1,0:T(8,128)}, u32[]{:S(2)}, u32[]{:S(2)}) collective-permute-start(f32[8,256]{1,0:T(8,128)S(1)} %concatenate.3.own_ref), channel_id=1, source_target_pairs={{16,0},{32,16},{48,32},{64,48},{80,64},{96,80},{112,96},{128,112},... | collective-permute-start | bytes 24584 | tf_op jit(solution)/shard_map/ppermute | solution.py:523
  11.7 1.9 %collective-permute-start = (f32[8,256]{1,0:T(8,128)S(1)}, f32[8,256]{1,0:T(8,128)}, u32[]{:S(2)}, u32[]{:S(2)}) collective-permute-start(f32[8,256]{1,0:T(8,128)S(1)} %concatenate.3.own_ref), channel_id=1, source_target_pairs={{0,16},{16,32},{32,48},{48,64},{64,80},{80,96},{96,112},{112,128},... | collective-permute-start | bytes 24584 | tf_op jit(solution)/shard_map/ppermute | solution.py:522
  13.6 0.7 convert_element_type.23
  14.3 0.6 pad.22.count_ref
  14.8 0.9 copy.45.neigh_ref
  15.8 1.8 %copy.46.e_in_ref = f32[1600,240]{1,0:T(8,128)S(1)} copy(f32[1600,240]{0,1:T(8,128)} %param.55) | data formatting | bytes 3072000 | tf_op args[12]
  17.5 0.0 copy-start.16
  17.5 0.0 copy-start.22
  17.6 0.0 copy-start.27
  17.6 0.0 copy-start.29
  17.6 1.8 %copy.47.w_in_ref = f32[1600,240]{1,0:T(8,128)S(1)} copy(f32[1600,240]{0,1:T(8,128)} %param.58) | data formatting | bytes 3072000 | tf_op args[15]
  19.4 0.0 collective-permute-done.1.upp_ref
  19.4 0.0 collective-permute-done.low_ref
  19.5 0.0 copy-start
  19.5 1.0 copy-done
  20.5 1.0 copy-done.1
  21.5 0.9 copy-done.17
  22.4 0.8 copy-done.20
  23.3 0.8 copy-done.21
  24.1 0.7 copy-done.23
  24.8 0.7 copy-done.24
  25.5 0.7 copy-done.25
  26.3 0.7 copy-done.26
  27.0 0.7 copy-done.28
  27.7 0.7 copy-done.30
  28.4 0.7 copy-done.31
  29.0 0.7 copy-done.32
  29.7 0.7 copy-done.33
  30.4 0.7 copy-done.34
  31.1 0.7 copy-done.35
  31.7 0.7 copy-done.36
  32.4 0.0 copy-start.6
  32.4 0.0 copy-start.7
  32.4 0.0 copy-start.8
  32.5 0.0 copy-start.9
  32.5 0.0 copy-start.10
  32.5 0.0 copy-start.11
  32.5 0.0 copy-start.12
  32.5 0.0 copy-start.13
  32.5 0.0 copy-start.14
  32.5 0.0 copy-start.15
  32.5 16.9 %atoms.1 = (f32[8,192]{1,0:T(8,128)S(1)}, f32[16,24,256]{2,1,0:T(8,128)S(1)}) custom-call(f32[8,256]{1,0:T(8,128)S(1)} %concatenate.3.own_ref, f32[8,256]{1,0:T(8,128)} %collective-permute-done.low_ref, f32[8,256]{1,0:T(8,128)} %collective-permute-done.1.upp_ref, f32[1,256]{1,0:T(1,128)S(1)} %copy-done.32, s32[1,192,64]{2,1,0:T(8,128)S(1)} %copy.45.neigh_ref, ...), custom_call_target="tpu_custom_call" | custom-call | tf_op jit(solution)/shard_map/atoms/pallas_call | solution.py:526
  49.5 0.0 copy-done.2
  49.5 0.0 copy-done.3
  49.5 0.0 copy-done.4
  49.5 0.0 copy-done.5
  49.5 0.0 copy-done.6
  49.5 0.0 copy-done.7
  49.5 0.0 copy-done.8
  49.5 0.0 copy-done.9
  49.6 0.0 copy-done.10
  49.6 0.0 copy-done.11
  49.6 0.0 copy-done.12
  49.6 0.0 copy-done.13
  49.6 0.0 copy-done.14
  49.6 0.0 copy-done.15
  49.6 0.0 copy-start.18
  49.6 0.0 copy-start.19
  49.6 57.8 %solve.1.in_ref = f32[16,24,256]{2,1,0:T(8,128)S(1)} custom-call(f32[16,24,256]{2,1,0:T(8,128)S(1)} %get-tuple-element.4.send_ref, bf16[256,384]{1,0:T(8,128)(2,1)S(1)} %copy-done.15, bf16[256,384]{1,0:T(8,128)(2,1)S(1)} %copy-done.14, bf16[512,256]{1,0:T(8,128)(2,1)S(1)} %copy-done.11, bf16[512,256]{1,0:T(8,128)(2,1)S(1)} %copy-done.10, ...), custom_call_target="tpu_custom_call" | custom-call | tf_op jit(solution)/shard_map/solve/pallas_call | solution.py:553
  107.5 0.0 copy-done.18
  107.5 1.7 %sample.1 = (f32[1,192]{1,0:T(1,128)}, f32[8,16,256]{2,1,0:T(8,128)}) custom-call(f32[16,24,256]{2,1,0:T(8,128)S(1)} %solve.1.in_ref, s32[1,192]{1,0:T(1,128)S(1)} %copy-done.29, s32[1,192]{1,0:T(1,128)S(1)} %copy-done.30, s32[1,192]{1,0:T(1,128)S(1)} %copy-done.31, f32[3,1,192]{2,1,0:T(1,128)S(1)} %copy-done.27, f32[8,192]{1,0:T(8,128)S(1)} %get-tuple-element.5.scal_ref, ...), custom_call_target="tpu_custom_call" | custom-call | tf_op jit(solution)/shard_map/sample/pallas_call | solution.py:583
  (31 shorter events, 0.1 us)
Async XLA Ops:
  2.9 16.5 %collective-permute-start.1 = (f32[8,256]{1,0:T(8,128)S(1)}, f32[8,256]{1,0:T(8,128)}, u32[]{:S(2)}, u32[]{:S(2)}) collective-permute-start(f32[8,256]{1,0:T(8,128)S(1)} %concatenate.3.own_ref), channel_id=1, source_target_pairs={{16,0},{32,16},{48,32},{64,48},{80,64},{96,80},{112,96},{128,112},... | collective-permute-start | bytes 24584 | tf_op jit(solution)/shard_map/ppermute | solution.py:523
  11.7 7.8 %collective-permute-start = (f32[8,256]{1,0:T(8,128)S(1)}, f32[8,256]{1,0:T(8,128)}, u32[]{:S(2)}, u32[]{:S(2)}) collective-permute-start(f32[8,256]{1,0:T(8,128)S(1)} %concatenate.3.own_ref), channel_id=1, source_target_pairs={{0,16},{16,32},{32,48},{48,64},{64,80},{80,96},{96,112},{112,128},... | collective-permute-start | bytes 24584 | tf_op jit(solution)/shard_map/ppermute | solution.py:522
  17.5 1.9 %copy-start.16 = (bf16[256,256]{1,0:T(8,128)(2,1)S(1)}, bf16[256,256]{1,0:T(8,128)(2,1)}, u32[]{:S(2)}) copy-start(bf16[256,256]{1,0:T(8,128)(2,1)} %constant.59.clone.zl_ref) | copy-start | bytes 393220
  17.5 1.9 %copy-start.22 = (f32[64,50]{1,0:T(8,128)S(1)}, f32[64,50]{1,0:T(8,128)}, u32[]{:S(2)}) copy-start(f32[64,50]{1,0:T(8,128)} %constant.53.clone.p2_ref) | copy-start | bytes 38404
  17.6 1.9 %copy-start.27 = (f32[3,1,192]{2,1,0:T(1,128)S(1)}, f32[3,1,192]{2,1,0:T(1,128)}, u32[]{:S(2)}) copy-start(f32[3,1,192]{2,1,0:T(1,128)} %frac_ref.3) | copy-start | bytes 6916
  17.6 1.9 %copy-start.29 = (s32[1,192]{1,0:T(1,128)S(1)}, s32[1,192]{1,0:T(1,128)}, u32[]{:S(2)}) copy-start(s32[1,192]{1,0:T(1,128)} %cx_ref.3) | copy-start | bytes 2308
  19.5 1.0 copy-start
  20.5 1.0 copy-start.1
  21.5 0.9 copy-start.17
  22.4 0.8 copy-start.20
  23.2 0.8 copy-start.21
  24.1 0.7 copy-start.23
  24.8 0.7 copy-start.24
  25.5 0.7 copy-start.25
  26.3 0.7 copy-start.26
  27.0 0.7 copy-start.28
  27.7 0.7 copy-start.30
  28.3 0.7 copy-start.31
  29.0 0.7 copy-start.32
  29.7 0.7 copy-start.33
  30.4 0.7 copy-start.34
  31.1 0.7 copy-start.35
  31.7 0.7 copy-start.36
  32.4 17.1 %copy-start.2 = (bf16[256,512]{1,0:T(8,128)(2,1)S(1)}, bf16[256,512]{1,0:T(8,128)(2,1)}, u32[]{:S(2)}) copy-start(bf16[256,512]{1,0:T(8,128)(2,1)} %constant.71.clone.lbl_ref) | copy-start | bytes 786436
  32.4 17.1 %copy-start.3 = (bf16[256,512]{1,0:T(8,128)(2,1)S(1)}, bf16[256,512]{1,0:T(8,128)(2,1)}, u32[]{:S(2)}) copy-start(bf16[256,512]{1,0:T(8,128)(2,1)} %constant.70.clone.lbh_ref) | copy-start | bytes 786436
  32.4 17.1 %copy-start.4 = (bf16[256,512]{1,0:T(8,128)(2,1)S(1)}, bf16[256,512]{1,0:T(8,128)(2,1)}, u32[]{:S(2)}) copy-start(bf16[256,512]{1,0:T(8,128)(2,1)} %constant.69.clone.rbl_ref) | copy-start | bytes 786436
  32.4 17.1 %copy-start.5 = (bf16[256,512]{1,0:T(8,128)(2,1)S(1)}, bf16[256,512]{1,0:T(8,128)(2,1)}, u32[]{:S(2)}) copy-start(bf16[256,512]{1,0:T(8,128)(2,1)} %constant.68.clone.rbh_ref) | copy-start | bytes 786436
  32.4 17.1 %copy-start.6 = (f32[256,256]{1,0:T(8,128)S(1)}, f32[256,256]{1,0:T(8,128)}, u32[]{:S(2)}) copy-start(f32[256,256]{1,0:T(8,128)} %constant.67.clone.ts_ref) | copy-start | bytes 786436
  32.4 17.1 %copy-start.7 = (f32[256,256]{1,0:T(8,128)S(1)}, f32[256,256]{1,0:T(8,128)}, u32[]{:S(2)}) copy-start(f32[256,256]{1,0:T(8,128)} %constant.66.clone.tc_ref) | copy-start | bytes 786436
  32.4 17.1 %copy-start.8 = (bf16[512,256]{1,0:T(8,128)(2,1)S(1)}, bf16[512,256]{1,0:T(8,128)(2,1)}, u32[]{:S(2)}) copy-start(bf16[512,256]{1,0:T(8,128)(2,1)} %constant.65.clone.rl_ref) | copy-start | bytes 786436
  32.5 17.1 %copy-start.9 = (bf16[512,256]{1,0:T(8,128)(2,1)S(1)}, bf16[512,256]{1,0:T(8,128)(2,1)}, u32[]{:S(2)}) copy-start(bf16[512,256]{1,0:T(8,128)(2,1)} %constant.64.clone.rh_ref) | copy-start | bytes 786436
  32.5 17.1 %copy-start.10 = (bf16[512,256]{1,0:T(8,128)(2,1)S(1)}, bf16[512,256]{1,0:T(8,128)(2,1)}, u32[]{:S(2)}) copy-start(bf16[512,256]{1,0:T(8,128)(2,1)} %constant.63.clone.ll_ref) | copy-start | bytes 786436
  32.5 17.1 %copy-start.11 = (bf16[512,256]{1,0:T(8,128)(2,1)S(1)}, bf16[512,256]{1,0:T(8,128)(2,1)}, u32[]{:S(2)}) copy-start(bf16[512,256]{1,0:T(8,128)(2,1)} %constant.62.clone.lh_ref) | copy-start | bytes 786436
  32.5 17.1 %copy-start.12 = (bf16[384,256]{1,0:T(8,128)(2,1)S(1)}, bf16[384,256]{1,0:T(8,128)(2,1)}, u32[]{:S(2)}) copy-start(bf16[384,256]{1,0:T(8,128)(2,1)} %constant.73.clone.ybl_ref) | copy-start | bytes 589828
  32.5 17.1 %copy-start.13 = (bf16[384,256]{1,0:T(8,128)(2,1)S(1)}, bf16[384,256]{1,0:T(8,128)(2,1)}, u32[]{:S(2)}) copy-start(bf16[384,256]{1,0:T(8,128)(2,1)} %constant.72.clone.ybh_ref) | copy-start | bytes 589828
  32.5 17.1 %copy-start.14 = (bf16[256,384]{1,0:T(8,128)(2,1)S(1)}, bf16[256,384]{1,0:T(8,128)(2,1)}, u32[]{:S(2)}) copy-start(bf16[256,384]{1,0:T(8,128)(2,1)} %constant.61.clone.yl_ref) | copy-start | bytes 589828
  32.5 17.1 %copy-start.15 = (bf16[256,384]{1,0:T(8,128)(2,1)S(1)}, bf16[256,384]{1,0:T(8,128)(2,1)}, u32[]{:S(2)}) copy-start(bf16[256,384]{1,0:T(8,128)(2,1)} %constant.60.clone.yh_ref) | copy-start | bytes 589828
  49.6 57.9 %copy-start.18 = (bf16[256,256]{1,0:T(8,128)(2,1)S(1)}, bf16[256,256]{1,0:T(8,128)(2,1)}, u32[]{:S(2)}) copy-start(bf16[256,256]{1,0:T(8,128)(2,1)} %constant.75.clone.zl_ref) | copy-start | bytes 393220
  49.6 57.8 %copy-start.19 = (bf16[256,256]{1,0:T(8,128)(2,1)S(1)}, bf16[256,256]{1,0:T(8,128)(2,1)}, u32[]{:S(2)}) copy-start(bf16[256,256]{1,0:T(8,128)(2,1)} %constant.74.clone.zh_ref) | copy-start | bytes 393220

commit v2 on v1

--- a/solution.py
+++ b/solution.py
@@ -105,13 +105,18 @@
     for row, feature in enumerate(second_rows()[:50]):
         placed[feature, row] = 1.0
     columns_second = np.tile(placed, (1, 3))
-    place = np.zeros(104, np.int32)
-    for row, feature in enumerate(third_rows()):
-        place[feature] = row
-    lanes = np.arange(13 * 128) // 16
-    spread = place[lanes].reshape(13, 128).astype(np.int32)
-    spread = np.concatenate([spread, np.zeros((3, 128), np.int32)])
-    return first, second, third, columns_first, columns_second, spread
+    table = np.zeros((296, 256), np.float32)
+    table[0:32, :25] = first
+    table[32:96, :50] = second
+    table[96:208, :100] = third
+    table[208:233, :96] = columns_first
+    table[240:290, :192] = columns_second
+    return table
+
+
+def places():
+    rows = third_rows()
+    return [rows.index(feature) for feature in range(100)]
 
 
 def halves(values):
@@ -171,79 +176,154 @@
     return wxy, wz
 
 
+LOADED = 20
+
+
 def atoms_kernel(
-    own_ref, low_ref, upp_ref, count_ref, neigh_ref,
-    cx_ref, cy_ref, cz_ref, frac_ref,
-    first_ref, second_ref, third_ref,
-    e_in_ref, e_hid_ref, e_out_ref, w_in_ref, w_hid_ref, w_out_ref, base_ref,
-    p1_ref, p2_ref, p3_ref, c1_ref, c2_ref, spread_ref, zh_ref, zl_ref,
+    pos_any, typ_any, snd_any, neigh_any, count_any, cx_any, cy_any, cz_any, frac_any,
+    first_any, second_any, third_any, e_in_any, e_hid_any, e_out_any, w_in_any, w_hid_any, w_out_any,
+    base_any, table_any, z_any,
     scal_ref, send_ref,
-    env_ref, moment_ref, desc_h_ref, desc_l_ref, w2_ref, w3_ref,
+    pos_ref, typ_ref, neigh_ref, count_ref, cx_ref, cy_ref, cz_ref, frac_ref,
+    first_ref, second_ref, third_ref, e_in_ref, e_hid_ref, e_out_ref, w_in_ref, w_hid_ref, w_out_ref,
+    base_ref, table_ref, z_ref,
+    low_pos, low_typ, low_snd, upp_pos, upp_typ, upp_snd,
+    env_ref, moment_ref, in_h_ref, in_l_ref, desc_h_ref, desc_l_ref, w2_ref, w3_ref,
+    load_sem, send_sem, recv_sem,
 ):
-    f1 = lax.dot_general(p1_ref[...], first_ref[...], NT, precision=HIGHEST)
+    b = lax.axis_index("brick")
+    s = lax.axis_index("slab")
+    below = (lax.rem(b + NB - 1, NB), s)
+    above = (lax.rem(b + 1, NB), s)
+    barrier = pltpu.get_barrier_semaphore()
+    for neighbour in (below, above):
+        pl.semaphore_signal(barrier, inc=1, device_id=neighbour, device_id_type=MESH)
+
+    sources = (
+        table_any, first_any, second_any, third_any, neigh_any, pos_any, typ_any, count_any,
+        e_in_any, w_in_any, e_hid_any, w_hid_any, e_out_any, w_out_any, base_any,
+        cx_any, cy_any, cz_any, frac_any, z_any,
+    )
+    targets = (
+        table_ref, first_ref, second_ref, third_ref, neigh_ref, pos_ref, typ_ref, count_ref,
+        e_in_ref, w_in_ref, e_hid_ref, w_hid_ref, e_out_ref, w_out_ref, base_ref,
+        cx_ref, cy_ref, cz_ref, frac_ref, z_ref,
+    )
+    loads = [
+        pltpu.make_async_copy(source, target, load_sem.at[i])
+        for i, (source, target) in enumerate(zip(sources, targets, strict=True))
+    ]
+    for load in loads:
+        load.start()
+
+    pl.semaphore_wait(barrier, 2)
+    ghosts = []
+    plan = (
+        (above, pos_any, low_pos), (above, typ_any, low_typ), (above, snd_any, low_snd),
+        (below, pos_any, upp_pos), (below, typ_any, upp_typ), (below, snd_any, upp_snd),
+    )
+    for i, (device, source, target) in enumerate(plan):
+        ghosts.append(
+            pltpu.make_async_remote_copy(
+                src_ref=source,
+                dst_ref=target,
+                send_sem=send_sem.at[i],
+                recv_sem=recv_sem.at[i],
+                device_id=device,
+                device_id_type=MESH,
+            )
+        )
+    for ghost in ghosts:
+        ghost.start()
+
+    for load in loads[:4]:
+        load.wait()
+    f1 = lax.dot_general(table_ref[0:32, 0:25], first_ref[...], NT, precision=HIGHEST)
     oxygen, hydrogen = f1[:, 0:1], f1[:, 1:2]
-    w2 = lax.dot_general(p2_ref[...], second_ref[...], NT, precision=HIGHEST)
-    w2 = lax.dot_general(w2, c1_ref[...], NN, precision=HIGHEST)
+    w2 = lax.dot_general(table_ref[32:96, 0:50], second_ref[...], NT, precision=HIGHEST)
+    w2 = lax.dot_general(w2, table_ref[208:233, 0:96], NN, precision=HIGHEST)
     high, low = halves(w2)
     slot = lanes_iota((64, 96)) // 32
     w2_ref[...] = jnp.where(slot == 1, low.astype(F32), high.astype(F32)).astype(BF16)
-    w3 = lax.dot_general(p3_ref[...], third_ref[...], NT, precision=HIGHEST)
-    w3 = lax.dot_general(w3, c2_ref[...], NN, precision=HIGHEST)
+    w3 = lax.dot_general(table_ref[96:208, 0:100], third_ref[...], NT, precision=HIGHEST)
+    w3 = lax.dot_general(w3, table_ref[240:290, 0:192], NN, precision=HIGHEST)
     high, low = halves(w3)
     slot = lanes_iota((112, 192)) // 64
     w3_ref[...] = jnp.where(slot == 1, low.astype(F32), high.astype(F32)).astype(BF16)
 
-    n = jnp.concatenate([neigh_ref[0, 0:96, :], neigh_ref[0, 96:192, :]], axis=1)
-    low_index = pick_index = (n - 96) & 127
+    for load in loads[4:10]:
+        load.wait()
+    high, low = halves(e_in_ref[...])
+    in_h_ref[0:240, :] = high
+    in_l_ref[0:240, :] = low
+    high, low = halves(w_in_ref[...])
+    in_h_ref[240:480, :] = high
+    in_l_ref[240:480, :] = low
+
+    n = jnp.concatenate(
+        [
+            neigh_ref[0, :, 0:128],
+            jnp.concatenate([neigh_ref[0, 0:32, 128:192], neigh_ref[0, 32:64, 128:192]], axis=1),
+        ],
+        axis=0,
+    )
+
+    def near(row):
+        return row[:, 0:128]
+
+    def far(row):
+        return jnp.concatenate([row[:, 128:192], row[:, 128:192]], axis=1)
+
+    def by_atom(row):
+        return jnp.concatenate(
+            [jnp.broadcast_to(near(row), (64, 128)), jnp.broadcast_to(far(row), (32, 128))], axis=0
+        )
+
+    own_index = (n - 96) & 127
     lower_index = n & 127
     upper_index = (n - 288) & 127
-    lane = lanes_iota((96, 128))
-    centre = rows_iota((96, 128)) + jnp.where(lane >= 64, 96, 0)
-    centre_index = centre & 127
-    ghosts_low = jnp.broadcast_to(low_ref[5:6, 0:128], (8, 128)).astype(jnp.int32)
-    ghosts_upp = jnp.broadcast_to(upp_ref[4:5, 0:128], (8, 128)).astype(jnp.int32)
-
-    def ghost_rows(ref, index):
-        near = jnp.take_along_axis(ref[:, 0:128], index & 127, axis=1, mode="promise_in_bounds")
-        far = jnp.take_along_axis(ref[:, 128:256], index & 127, axis=1, mode="promise_in_bounds")
-        return jnp.where(index < 128, near, far)
-
-    lower = ghost_rows(low_ref, ghosts_low)
-    upper = ghost_rows(upp_ref, ghosts_upp)
+    row96 = rows_iota((96, 128))
+    slot = jnp.where(row96 < 64, row96, row96 - 64 + jnp.where(lanes_iota((96, 128)) < 64, 0, 32))
+    live = slot < by_atom(count_ref[...])
+
+    for ghost in ghosts:
+        ghost.wait_recv()
+
+    low_snd_row = low_snd[...]
+    upp_snd_row = upp_snd[...]
+    low_list = jnp.concatenate([low_snd_row[:, 96:192], low_snd_row[:, 0:32]], axis=1)
+    upp_list = upp_snd_row[:, 0:128]
+
+    def ghost_row(row, index):
+        index = jnp.broadcast_to(index, (8, 128))
+        value = jnp.where(index < 128, pick(near(row), index & 127), pick(far(row), index & 127))
+        return value[0:1]
+
     gathered = []
     for c in range(4):
-        value = pick(own_ref[c : c + 1, 0:128], pick_index)
-        value = jnp.where(n < 224, value, pick(own_ref[c : c + 1, 128:256], pick_index))
-        value = jnp.where(n < 96, pick(lower[c : c + 1], lower_index), value)
-        value = jnp.where(n >= 288, pick(upper[c : c + 1], upper_index), value)
+        own = pos_ref[c] if c < 3 else typ_ref[...].astype(F32)
+        low = low_pos[c] if c < 3 else low_typ[...].astype(F32)
+        upp = upp_pos[c] if c < 3 else upp_typ[...].astype(F32)
+        value = jnp.where(n < 224, pick(near(own), own_index), pick(far(own), own_index))
+        value = jnp.where(n < 96, pick(ghost_row(low, low_list), lower_index), value)
+        value = jnp.where(n >= 288, pick(ghost_row(upp, upp_list), upper_index), value)
+        if c < 3:
+            value = value - by_atom(own)
         gathered.append(value)
-    offsets = []
-    for c in range(3):
-        here = jnp.where(
-            centre < 128,
-            pick(own_ref[c : c + 1, 0:128], centre_index),
-            pick(own_ref[c : c + 1, 128:256], centre_index),
-        )
-        offsets.append(gathered[c] - here)
-    total = jnp.where(
-        centre < 128,
-        pick(count_ref[0:1, 0:128], centre_index),
-        pick(count_ref[0:1, 128:256], centre_index),
-    )
-    squared = offsets[0] * offsets[0] + offsets[1] * offsets[1] + offsets[2] * offsets[2]
-    smooth = jnp.where((lane & 63).astype(F32) < total, 1.0 / (1.0 + squared), 0.0)
+    squared = gathered[0] * gathered[0] + gathered[1] * gathered[1] + gathered[2] * gathered[2]
+    smooth = jnp.where(live, 1.0 / (1.0 + squared), 0.0)
     env_ref[0] = smooth
     for c in range(3):
-        env_ref[c + 1] = smooth * offsets[c]
+        env_ref[c + 1] = smooth * gathered[c]
     env_ref[4] = gathered[3]
+    moment_ref[...] = jnp.zeros_like(moment_ref)
 
     oxygen_wide = jnp.broadcast_to(oxygen, (32, 128))
     hydrogen_wide = jnp.broadcast_to(hydrogen, (32, 128))
-    row8 = rows_iota((8, 128))
-    left8 = lanes_iota((8, 128)) < 64
 
     def chunk(step, carry):
         at = pl.multiple_of(step * 8, 8)
+        tile = step // 8
         first = []
         for r in range(8):
             sm = env_ref[0, pl.ds(at + r, 1), :]
@@ -258,63 +338,52 @@
         high, low = halves(padded)
         third = dot(w3_ref[...], jnp.concatenate([high, high, low], axis=0))
         third = jnp.tanh(third[:104]) + jnp.concatenate([second[:48], second], axis=0)
-        third = jnp.concatenate([third, jnp.zeros((8, 1024), F32)], axis=0)
-        third = halves(third)
-        rows = []
         for c in range(4):
-            value = env_ref[c, pl.ds(at, 8), :] * (1.0 / 64.0)
-            for half in range(2):
-                side = left8 if half == 0 else jnp.logical_not(left8)
-                kept = jnp.where(side, value, 0.0)
-                rows.append(
-                    jnp.concatenate([jnp.where(row8 == r, kept, 0.0) for r in range(8)], axis=1)
-                )
-        rows = halves(jnp.concatenate(rows, axis=0))
-        both = dot(jnp.concatenate(rows, axis=0), third[0], NT)
-        moments = both[:64] + both[64:] + dot(rows[0], third[1], NT)
-        for c in range(4):
-            for half in range(2):
-                k = (c * 2 + half) * 8
-                moment_ref[c, pl.ds(at + half * 96, 8), 0:112] = moments[k : k + 8]
+            total = None
+            for r in range(8):
+                part = third[:, r * 128 : (r + 1) * 128] * env_ref[c, pl.ds(at + r, 1), :]
+                total = part if total is None else total + part
+            moment_ref[tile, c] += total
         return carry
 
     lax.fori_loop(0, 12, chunk, 0)
 
-    lane_a = lanes_iota((A, 128))
-    moments = [jnp.where(lane_a < 104, moment_ref[c], 0.0) for c in range(4)]
-    factors = [
-        jnp.take_along_axis(m, lane_a & 15, axis=1, mode="promise_in_bounds") for m in moments
-    ]
-    for j in range(13):
-        index = jnp.broadcast_to(spread_ref[j : j + 1, :], (A, 128))
-        value = None
-        for c in range(4):
-            term = jnp.take_along_axis(moments[c], index, axis=1, mode="promise_in_bounds")
-            term = term * factors[c]
-            value = term if value is None else value + term
-        high, low = halves(value)
-        desc_h_ref[:, j * 128 : (j + 1) * 128] = high
-        desc_l_ref[:, j * 128 : (j + 1) * 128] = low
-
-    def network(in_ref, hid_ref, out_ref):
-        weight = halves(in_ref[...])
-        hidden = jnp.tanh(dot3((desc_h_ref[:, 0:1600], desc_l_ref[:, 0:1600]), weight))
+    for c in range(4):
+        moment_ref[0, c] = moment_ref[0, c] * (1.0 / 64.0)
+        value = moment_ref[1, c]
+        moment_ref[1, c] = (value + pltpu.roll(value, 64, 1)) * (1.0 / 64.0)
+    for tile in range(2):
+        factors = [moment_ref[tile, c, 0:16, :] for c in range(4)]
+        for m, place in enumerate(places()):
+            value = None
+            for c in range(4):
+                term = moment_ref[tile, c, place : place + 1, :] * factors[c]
+                value = term if value is None else value + term
+            high, low = halves(value)
+            desc_h_ref[m * 16 : m * 16 + 16, tile * 128 : (tile + 1) * 128] = high
+            desc_l_ref[m * 16 : m * 16 + 16, tile * 128 : (tile + 1) * 128] = low
+
+    both = jnp.tanh(dot3((in_h_ref[...], in_l_ref[...]), (desc_h_ref[...], desc_l_ref[...])))
+    for load in loads[10:]:
+        load.wait()
+
+    def network(hidden, hid_ref, out_ref):
         for layer in range(2):
             hidden = jnp.tanh(dot3(halves(hidden), halves(hid_ref[layer]))) + hidden
         row = jnp.broadcast_to(out_ref[...], (16, 240))
-        return dot3(halves(row), halves(hidden), NT)[0:1]
-
-    energy = network(e_in_ref, e_hid_ref, e_out_ref)
-    shift = network(w_in_ref, w_hid_ref, w_out_ref)
-    charge = jnp.where(own_ref[3:4, 0:A] > 0.5, base_ref[1], base_ref[0]) + shift
+        return dot3(halves(row), halves(hidden), NT)[0:1, 0:A]
+
+    energy = network(both[:240].T, e_hid_ref, e_out_ref)
+    shift = network(both[240:].T, w_hid_ref, w_out_ref)
+    charge = jnp.where(typ_ref[...] == 1, base_ref[0:1, 1:2], base_ref[0:1, 0:1]) + shift
     scal_ref[...] = jnp.concatenate([energy, charge, jnp.zeros((6, A), F32)], axis=0)
 
     wxy, wz = spreads(cx_ref, cy_ref, cz_ref, frac_ref)
     grid = dot3(halves(wxy), halves(wz * charge), NT)
-    spectrum = dot3(halves(grid), (zh_ref[...], zl_ref[...]))
+    spectrum = dot3(halves(grid), (z_ref[0:256, :], z_ref[256:512, :]))
     chunk_lane = lanes_iota((WY, 128)) // 16
-    for s in range(NS):
-        tile, chunk_from = divmod(s, 8)
+    for s_to in range(NS):
+        tile, chunk_from = divmod(s_to, 8)
         for half in range(2):
             out = jnp.zeros((WY, 128), F32)
             for x in range(8 * half, min(8 * half + 8, WX)):
@@ -323,7 +392,9 @@
                 if shift_by:
                     source = pltpu.roll(source, shift_by, 1)
                 out = jnp.where(chunk_lane == x % 8, source, out)
-            send_ref[s, :, half * 128 : (half + 1) * 128] = out
+            send_ref[s_to, :, half * 128 : (half + 1) * 128] = out
+    for ghost in ghosts:
+        ghost.wait_send()
 
 
 def solve_kernel(
@@ -495,7 +566,7 @@
 
 
 VMEM = pl.BlockSpec(memory_space=pltpu.VMEM)
-SMEM = pl.BlockSpec(memory_space=pltpu.SMEM)
+HBM = pl.BlockSpec(memory_space=pltpu.HBM)
 
 
 def per_device(
@@ -504,50 +575,64 @@
     wannier_in, wannier_hidden, wannier_out, charge_base,
 ):
     tables = transform_tables()
-    embedding = embedding_tables()
-
-    def wide(rows):
-        return jnp.pad(rows, ((0, 0), (0, 256 - rows.shape[1])))
-
-    own = jnp.concatenate(
-        [
-            wide(positions[:, 0]),
-            wide(types.astype(F32)),
-            wide(send_index[:, :96].astype(F32)),
-            wide(send_index[:, 96:].astype(F32)),
-            jnp.zeros((2, 256), F32),
-        ],
-        axis=0,
-    )
-    lower = lax.ppermute(own, "brick", [(i, (i + 1) % NB) for i in range(NB)])
-    upper = lax.ppermute(own, "brick", [((i + 1) % NB, i) for i in range(NB)])
-    count = wide(neighbour_count.astype(F32))
-
     scalars, send = pl.pallas_call(
         atoms_kernel,
         out_shape=(
             jax.ShapeDtypeStruct((8, A), F32),
             jax.ShapeDtypeStruct((NS, WY, NG), F32),
         ),
-        in_specs=[VMEM] * 18 + [SMEM] + [VMEM] * 8,
+        in_specs=[HBM] * 21,
         out_specs=(VMEM, VMEM),
         scratch_shapes=[
+            pltpu.VMEM((3, 1, A), F32),
+            pltpu.VMEM((1, A), jnp.int32),
+            pltpu.VMEM((1, 64, A), jnp.int32),
+            pltpu.VMEM((1, A), jnp.int32),
+            pltpu.VMEM((1, A), jnp.int32),
+            pltpu.VMEM((1, A), jnp.int32),
+            pltpu.VMEM((1, A), jnp.int32),
+            pltpu.VMEM((3, 1, A), F32),
+            pltpu.VMEM((2, 25), F32),
+            pltpu.VMEM((25, 50), F32),
+            pltpu.VMEM((50, 100), F32),
+            pltpu.VMEM((240, 1600), F32),
+            pltpu.VMEM((2, 240, 240), F32),
+            pltpu.VMEM((1, 240), F32),
+            pltpu.VMEM((240, 1600), F32),
+            pltpu.VMEM((2, 240, 240), F32),
+            pltpu.VMEM((1, 240), F32),
+            pltpu.VMEM((1, 2), F32),
+            pltpu.VMEM((296, 256), F32),
+            pltpu.VMEM((512, 256), BF16),
+            pltpu.VMEM((3, 1, A), F32),
+            pltpu.VMEM((1, A), jnp.int32),
+            pltpu.VMEM((1, A), jnp.int32),
+            pltpu.VMEM((3, 1, A), F32),
+            pltpu.VMEM((1, A), jnp.int32),
+            pltpu.VMEM((1, A), jnp.int32),
             pltpu.VMEM((5, 96, 128), F32),
-            pltpu.VMEM((4, A, 128), F32),
-            pltpu.VMEM((A, 1664), BF16),
-            pltpu.VMEM((A, 1664), BF16),
+            pltpu.VMEM((2, 4, 104, 128), F32),
+            pltpu.VMEM((480, 1600), BF16),
+            pltpu.VMEM((480, 1600), BF16),
+            pltpu.VMEM((1600, 256), BF16),
+            pltpu.VMEM((1600, 256), BF16),
             pltpu.VMEM((64, 96), BF16),
             pltpu.VMEM((112, 192), BF16),
+            pltpu.SemaphoreType.DMA((LOADED,)),
+            pltpu.SemaphoreType.DMA((6,)),
+            pltpu.SemaphoreType.DMA((6,)),
         ],
-        compiler_params=pltpu.CompilerParams(vmem_limit_bytes=48 * MIB),
+        compiler_params=pltpu.CompilerParams(
+            collective_id=2, has_side_effects=True, vmem_limit_bytes=60 * MIB
+        ),
         name="atoms",
     )(
-        own, lower, upper, count, neighbours,
+        positions, types, send_index, jnp.swapaxes(neighbours, 1, 2), neighbour_count,
         cell_x, cell_y, cell_z, spline_fraction,
         embed_first, embed_second, embed_third,
-        energy_in, energy_hidden, energy_out.reshape(1, -1),
-        wannier_in, wannier_hidden, wannier_out.reshape(1, -1), charge_base,
-        *embedding, *tables["z"],
+        energy_in.T, energy_hidden, energy_out.reshape(1, -1),
+        wannier_in.T, wannier_hidden, wannier_out.reshape(1, -1), charge_base.reshape(1, 2),
+        embedding_tables(), np.concatenate(tables["z"]),
     )
 
     received = pl.pallas_call(

time: 110 us -> 84.7 us (0.77)
  the two profiles are of different devices: /device:TPU:1 before, /device:TPU:16 now
where the time goes in v2:
time: 84.7 us; the launch traced here: 84.5 us
  Pallas kernels  82.4 us (97%)
  local copies, waits for them, and re-layouts  1.12 us (1%)
  between operations  0.97 us (1%)
    pallas_call x1, Pallas kernels, per_device(): pl.pallas_call(solve_kernel, out_shape=jax.ShapeDtypeStruct((NS, WY, NG),...  62.8 us
    pallas_call x1, Pallas kernels, per_device(): pl.pallas_call(atoms_kernel, out_shape=(jax.ShapeDtypeStruct((8, A), F32)...  18 us

profile of v2, /device:TPU:16, one launch (start us, length us, event | category | flops | bytes accessed | tf_op | source)
XLA Modules:
  0.0 84.5 jit_solution(15793880788453491049)
XLA Ops:
  0.6 0.0 copy-start.1
  0.6 0.0 copy-start.2
  0.7 0.0 copy-start.3
  0.7 0.0 copy-start.4
  0.7 0.0 copy-start.5
  0.7 0.0 copy-start.6
  0.7 0.0 copy-start.7
  0.7 0.0 copy-start.8
  0.7 0.0 copy-start.9
  0.7 0.0 copy-start.10
  0.8 0.0 copy-start.11
  0.8 0.0 copy-start.12
  0.8 0.0 copy-start.13
  0.8 0.0 copy-start.14
  0.8 18.0 %atoms.1 = (f32[8,192]{1,0:T(8,128)}, f32[16,24,256]{2,1,0:T(8,128)}) custom-call(f32[3,1,192]{2,1,0:T(1,128)} %pos_any.1, s32[1,192]{1,0:T(1,128)} %typ_any.1, s32[1,192]{1,0:T(1,128)} %snd_any.1, s32[1,64,192]{2,1,0:T(8,128)} %bitcast.8, s32[1,192]{1,0:T(1,128)} %count_any.1, s32[1,192]{1,0:T(1,128)} %cx_ref.1, s32[1,192]{1,0:T(1,128)} %cy_ref.1, ...), custom_call_target="tpu_custom_call" | custom-call | tf_op jit(solution)/shard_map/atoms/pallas_call | solution.py:578
  18.8 0.0 copy-done.1
  18.8 0.0 copy-done.2
  18.8 0.0 copy-done.3
  18.8 0.0 copy-done.4
  18.8 0.0 copy-done.5
  18.8 0.0 copy-done.6
  18.8 0.0 copy-done.7
  18.8 0.0 copy-done.8
  18.9 0.0 copy-done.9
  18.9 0.0 copy-done.10
  18.9 0.0 copy-done.11
  18.9 0.0 copy-done.12
  18.9 0.0 copy-done.13
  18.9 0.0 copy-done.14
  18.9 0.0 copy-start
  18.9 1.0 %copy-done = f32[16,24,256]{2,1,0:T(8,128)S(1)} copy-done((f32[16,24,256]{2,1,0:T(8,128)S(1)}, f32[16,24,256]{2,1,0:T(8,128)}, u32[]{:S(2)}) %copy-start) | copy-done | bytes 393240
  19.9 0.0 copy-start.15
  19.9 0.0 copy-start.16
  19.9 0.0 copy-start.17
  19.9 0.0 copy-start.18
  19.9 0.0 copy-start.19
  19.9 0.0 copy-start.20
  19.9 0.0 copy-start.21
  20.0 62.8 %solve.1.in_ref = f32[16,24,256]{2,1,0:T(8,128)S(1)} custom-call(f32[16,24,256]{2,1,0:T(8,128)S(1)} %copy-done, bf16[256,384]{1,0:T(8,128)(2,1)S(1)} %copy-done.14, bf16[256,384]{1,0:T(8,128)(2,1)S(1)} %copy-done.13, bf16[512,256]{1,0:T(8,128)(2,1)S(1)} %copy-done.10, bf16[512,256]{1,0:T(8,128)(2,1)S(1)} %copy-done.9, bf16[512,256]{1,0:T(8,128)(2,1)S(1)} %copy-done.8, ...), custom_call_target="tpu_custom_call" | custom-call | tf_op jit(solution)/shard_map/solve/pallas_call | solution.py:638
  82.8 0.0 copy-done.15
  82.8 0.0 copy-done.16
  82.8 0.0 copy-done.17
  82.8 0.0 copy-done.18
  82.8 0.0 copy-done.19
  82.8 0.0 copy-done.20
  82.8 0.0 copy-done.21
  82.9 1.7 %sample.1 = (f32[1,192]{1,0:T(1,128)}, f32[8,16,256]{2,1,0:T(8,128)}) custom-call(f32[16,24,256]{2,1,0:T(8,128)S(1)} %solve.1.in_ref, s32[1,192]{1,0:T(1,128)S(1)} %copy-done.19, s32[1,192]{1,0:T(1,128)S(1)} %copy-done.20, s32[1,192]{1,0:T(1,128)S(1)} %copy-done.21, f32[3,1,192]{2,1,0:T(1,128)S(1)} %copy-done.17, f32[8,192]{1,0:T(8,128)S(1)} %copy-done.18, ...), custom_call_target="tpu_custom_call" | custom-call | tf_op jit(solution)/shard_map/sample/pallas_call | solution.py:668
Async XLA Ops:
  0.6 18.1 %copy-start.1 = (bf16[256,512]{1,0:T(8,128)(2,1)S(1)}, bf16[256,512]{1,0:T(8,128)(2,1)}, u32[]{:S(2)}) copy-start(bf16[256,512]{1,0:T(8,128)(2,1)} %constant.49.clone.lbl_ref) | copy-start | bytes 786436
  0.6 18.1 %copy-start.2 = (bf16[256,512]{1,0:T(8,128)(2,1)S(1)}, bf16[256,512]{1,0:T(8,128)(2,1)}, u32[]{:S(2)}) copy-start(bf16[256,512]{1,0:T(8,128)(2,1)} %constant.48.clone.lbh_ref) | copy-start | bytes 786436
  0.7 18.1 %copy-start.3 = (bf16[256,512]{1,0:T(8,128)(2,1)S(1)}, bf16[256,512]{1,0:T(8,128)(2,1)}, u32[]{:S(2)}) copy-start(bf16[256,512]{1,0:T(8,128)(2,1)} %constant.47.clone.rbl_ref) | copy-start | bytes 786436
  0.7 18.1 %copy-start.4 = (bf16[256,512]{1,0:T(8,128)(2,1)S(1)}, bf16[256,512]{1,0:T(8,128)(2,1)}, u32[]{:S(2)}) copy-start(bf16[256,512]{1,0:T(8,128)(2,1)} %constant.46.clone.rbh_ref) | copy-start | bytes 786436
  0.7 18.1 %copy-start.5 = (f32[256,256]{1,0:T(8,128)S(1)}, f32[256,256]{1,0:T(8,128)}, u32[]{:S(2)}) copy-start(f32[256,256]{1,0:T(8,128)} %constant.45.clone.ts_ref) | copy-start | bytes 786436
  0.7 18.1 %copy-start.6 = (f32[256,256]{1,0:T(8,128)S(1)}, f32[256,256]{1,0:T(8,128)}, u32[]{:S(2)}) copy-start(f32[256,256]{1,0:T(8,128)} %constant.44.clone.tc_ref) | copy-start | bytes 786436
  0.7 18.1 %copy-start.7 = (bf16[512,256]{1,0:T(8,128)(2,1)S(1)}, bf16[512,256]{1,0:T(8,128)(2,1)}, u32[]{:S(2)}) copy-start(bf16[512,256]{1,0:T(8,128)(2,1)} %constant.43.clone.rl_ref) | copy-start | bytes 786436
  0.7 18.1 %copy-start.8 = (bf16[512,256]{1,0:T(8,128)(2,1)S(1)}, bf16[512,256]{1,0:T(8,128)(2,1)}, u32[]{:S(2)}) copy-start(bf16[512,256]{1,0:T(8,128)(2,1)} %constant.42.clone.rh_ref) | copy-start | bytes 786436
  0.7 18.1 %copy-start.9 = (bf16[512,256]{1,0:T(8,128)(2,1)S(1)}, bf16[512,256]{1,0:T(8,128)(2,1)}, u32[]{:S(2)}) copy-start(bf16[512,256]{1,0:T(8,128)(2,1)} %constant.41.clone.ll_ref) | copy-start | bytes 786436
  0.7 18.1 %copy-start.10 = (bf16[512,256]{1,0:T(8,128)(2,1)S(1)}, bf16[512,256]{1,0:T(8,128)(2,1)}, u32[]{:S(2)}) copy-start(bf16[512,256]{1,0:T(8,128)(2,1)} %constant.40.clone.lh_ref) | copy-start | bytes 786436
  0.8 18.1 %copy-start.11 = (bf16[384,256]{1,0:T(8,128)(2,1)S(1)}, bf16[384,256]{1,0:T(8,128)(2,1)}, u32[]{:S(2)}) copy-start(bf16[384,256]{1,0:T(8,128)(2,1)} %constant.51.clone.ybl_ref) | copy-start | bytes 589828
  0.8 18.1 %copy-start.12 = (bf16[384,256]{1,0:T(8,128)(2,1)S(1)}, bf16[384,256]{1,0:T(8,128)(2,1)}, u32[]{:S(2)}) copy-start(bf16[384,256]{1,0:T(8,128)(2,1)} %constant.50.clone.ybh_ref) | copy-start | bytes 589828
  0.8 18.1 %copy-start.13 = (bf16[256,384]{1,0:T(8,128)(2,1)S(1)}, bf16[256,384]{1,0:T(8,128)(2,1)}, u32[]{:S(2)}) copy-start(bf16[256,384]{1,0:T(8,128)(2,1)} %constant.39.clone.yl_ref) | copy-start | bytes 589828
  0.8 18.1 %copy-start.14 = (bf16[256,384]{1,0:T(8,128)(2,1)S(1)}, bf16[256,384]{1,0:T(8,128)(2,1)}, u32[]{:S(2)}) copy-start(bf16[256,384]{1,0:T(8,128)(2,1)} %constant.38.clone.yh_ref) | copy-start | bytes 589828
  18.9 1.0 %copy-start = (f32[16,24,256]{2,1,0:T(8,128)S(1)}, f32[16,24,256]{2,1,0:T(8,128)}, u32[]{:S(2)}) copy-start(f32[16,24,256]{2,1,0:T(8,128)} %get-tuple-element.4.send_ref) | copy-start | bytes 1179652
  19.9 62.9 %copy-start.15 = (bf16[256,256]{1,0:T(8,128)(2,1)S(1)}, bf16[256,256]{1,0:T(8,128)(2,1)}, u32[]{:S(2)}) copy-start(bf16[256,256]{1,0:T(8,128)(2,1)} %constant.53.clone.zl_ref) | copy-start | bytes 393220
  19.9 62.9 %copy-start.16 = (bf16[256,256]{1,0:T(8,128)(2,1)S(1)}, bf16[256,256]{1,0:T(8,128)(2,1)}, u32[]{:S(2)}) copy-start(bf16[256,256]{1,0:T(8,128)(2,1)} %constant.52.clone.zh_ref) | copy-start | bytes 393220
  19.9 62.9 %copy-start.17 = (f32[3,1,192]{2,1,0:T(1,128)S(1)}, f32[3,1,192]{2,1,0:T(1,128)}, u32[]{:S(2)}) copy-start(f32[3,1,192]{2,1,0:T(1,128)} %frac_ref.1) | copy-start | bytes 6916
  19.9 62.9 %copy-start.18 = (f32[8,192]{1,0:T(8,128)S(1)}, f32[8,192]{1,0:T(8,128)}, u32[]{:S(2)}) copy-start(f32[8,192]{1,0:T(8,128)} %get-tuple-element.5.scal_ref) | copy-start | bytes 18436
  19.9 62.9 %copy-start.19 = (s32[1,192]{1,0:T(1,128)S(1)}, s32[1,192]{1,0:T(1,128)}, u32[]{:S(2)}) copy-start(s32[1,192]{1,0:T(1,128)} %cx_ref.1) | copy-start | bytes 2308
  19.9 62.9 %copy-start.20 = (s32[1,192]{1,0:T(1,128)S(1)}, s32[1,192]{1,0:T(1,128)}, u32[]{:S(2)}) copy-start(s32[1,192]{1,0:T(1,128)} %cy_ref.1) | copy-start | bytes 2308
  19.9 62.9 %copy-start.21 = (s32[1,192]{1,0:T(1,128)S(1)}, s32[1,192]{1,0:T(1,128)}, u32[]{:S(2)}) copy-start(s32[1,192]{1,0:T(1,128)} %cz_ref.1) | copy-start | bytes 2308

commit v3 on v2

v3 whole, which is shorter than its diff:
```python
import math

import jax
import jax.numpy as jnp
import numpy as np
from jax import lax
from jax.experimental import pallas as pl
from jax.experimental.pallas import tpu as pltpu
from jax.sharding import PartitionSpec as P

NG = 256
A = 192
NB = 32
NS = 16
CX = 8
CY = 16
MIB = 1024 * 1024
F32 = jnp.float32
BF16 = jnp.bfloat16
HIGHEST = lax.Precision.HIGHEST
MESH = pl.DeviceIdType.MESH

NN = (((1,), (0,)), ((), ()))
NT = (((1,), (1,)), ((), ()))


def split(table):
    table = np.asarray(table, np.float64)
    high = np.asarray(table, np.float32).astype(jnp.bfloat16)
    low = (table - high.astype(np.float64)).astype(np.float32).astype(jnp.bfloat16)
    return high, low


def real_basis():
    n = np.arange(NG)[:, None]
    j = np.arange(NG)[None, :]
    phase = 2.0 * np.pi * ((n * j) % NG) / NG
    basis = np.where(j <= NG // 2, np.cos(phase), np.sin(phase)) * math.sqrt(2.0 / NG)
    basis[:, 0] = 1.0 / 16.0
    basis[:, NG // 2] = np.where(np.arange(NG) % 2 == 0, 1.0, -1.0) / 16.0
    return basis


def transform_tables():
    basis = real_basis()
    b = np.arange(NB)
    angle = 2.0 * np.pi * np.outer(b, b) / NB
    eye8 = np.eye(8)
    left = np.concatenate([np.kron(np.cos(angle), eye8), np.kron(np.sin(angle), eye8)], axis=0)
    xi = np.arange(8)
    small = 2.0 * np.pi * np.outer(xi, xi) / 8
    eye16 = np.eye(16)
    cos_m = np.kron(np.cos(small), eye16)
    sin_m = np.kron(np.sin(small), eye16)
    right = np.block([[cos_m, -sin_m], [sin_m, cos_m]])
    high, low = zip(*(split(table) for table in (basis, basis.T, left, right)), strict=True)
    twist = 2.0 * np.pi * np.repeat(b, 8)[:, None] * np.repeat(xi, 16)[None, :] / NG
    twist = np.concatenate([np.cos(twist), np.sin(twist)]).astype(np.float32)
    return np.concatenate(high), np.concatenate(low), twist


def second_rows():
    rows = list(range(24)) + list(range(25, 49)) + [24, 49, 24, 49]
    return rows


def third_rows():
    second = second_rows()
    return [f for f in second[:48]] + [50 + f for f in second[:48]] + [24, 49, 74, 99]


def one_hot(rows, height, width):
    table = np.zeros((height, width), np.float32)
    for row, feature in enumerate(rows):
        table[row, feature] = 1.0
    return table


def embedding_tables():
    first = one_hot(list(range(25)) + [24, 24, 24], 32, 25)
    second = one_hot(second_rows(), 64, 50)
    third = one_hot(third_rows(), 112, 100)
    columns_first = np.tile(np.eye(25, 32, dtype=np.float32), (1, 3))
    placed = np.zeros((50, 64), np.float32)
    for row, feature in enumerate(second_rows()[:50]):
        placed[feature, row] = 1.0
    columns_second = np.tile(placed, (1, 3))
    table = np.zeros((296, 256), np.float32)
    table[0:32, :25] = first
    table[32:96, :50] = second
    table[96:208, :100] = third
    table[208:233, :96] = columns_first
    table[240:290, :192] = columns_second
    return table


def places():
    rows = third_rows()
    return [rows.index(feature) for feature in range(100)]


def halves(values):
    high = values.astype(BF16)
    low = (values - high.astype(F32)).astype(BF16)
    return high, low


def dot(a, b, dims=NN):
    return lax.dot_general(a, b, dims, preferred_element_type=F32)


def dot3(a, b, dims=NN):
    return dot(a[0], b[0], dims) + (dot(a[0], b[1], dims) + dot(a[1], b[0], dims))


def dot3_narrow(a, b):
    both = dot(a[0], jnp.concatenate([b[0], b[1]], axis=1))
    return both[:, :128] + (both[:, 128:] + dot(a[1], b[0]))


def lanes_iota(shape):
    return lax.broadcasted_iota(jnp.int32, shape, 1)


def rows_iota(shape):
    return lax.broadcasted_iota(jnp.int32, shape, 0)


def pick(row, index):
    table = jnp.broadcast_to(row, index.shape)
    return jnp.take_along_axis(table, index, axis=1, mode="promise_in_bounds")


def spline_rows(u):
    cubed = u * u * u
    square = u * u
    rest = 1.0 - u
    return (
        rest * rest * rest / 6.0,
        (3.0 * cubed - 6.0 * square + 4.0) / 6.0,
        (-3.0 * cubed + 3.0 * square + 3.0 * u + 1.0) / 6.0,
        cubed / 6.0,
    )


def place_rows(start, weights, height, wrap):
    offset = rows_iota((height, A)) - start
    if wrap:
        offset = offset & (wrap - 1)
    result = jnp.zeros((height, A), F32)
    for step in range(4):
        result = jnp.where(offset == step, weights[step], result)
    return result


LOADED = 22


def kernel(
    pos_any, typ_any, snd_any, neigh_any, count_any, cx_any, cy_any, cz_any, frac_any,
    first_any, second_any, third_any, e_in_any, e_hid_any, e_out_any, w_in_any, w_hid_any, w_out_any,
    base_any, table_any, high_any, low_any, twist_any,
    energy_ref, pot_any,
    pos_ref, typ_ref, neigh_ref, count_ref, cx_ref, cy_ref, cz_ref, frac_ref,
    first_ref, second_ref, third_ref, e_in_ref, e_hid_ref, e_out_ref, w_in_ref, w_hid_ref, w_out_ref,
    base_ref, table_ref, high_ref, low_ref, twist_ref,
    low_pos, low_typ, low_snd, upp_pos, upp_typ, upp_snd,
    env_ref, moment_ref, in_h_ref, in_l_ref, desc_h_ref, desc_l_ref, w2_ref, w3_ref,
    charge_ref, charges_ref, wxy_ref, wz_h_ref, wz_l_ref, green_ref,
    out1, in1, out2, in2, out3, in3, out4, in4, modes_ref, pot_ref, part_ref, back_ref,
    load_sem, pot_sem, ghost_send, ghost_recv, cell_send, cell_recv, charge_send, charge_recv,
    part_send, part_recv, send1, recv1, send2, recv2, send3, recv3, send4, recv4,
):
    b = lax.axis_index("brick")
    s = lax.axis_index("slab")
    b_up, b_down = lax.rem(b + 1, NB), lax.rem(b + NB - 1, NB)
    s_up, s_down = lax.rem(s + 1, NS), lax.rem(s + NS - 1, NS)
    below, above = (b_down, s), (b_up, s)
    shifts = ((0, 0), (1, 0), (0, 1), (1, 1))
    onward = ((b, s), (b_up, s), (b, s_up), (b_up, s_up))
    origin = ((b, s), (b_down, s), (b, s_down), (b_down, s_down))

    barrier = pltpu.get_barrier_semaphore()

    def greet_slab(i, carry):
        pl.semaphore_signal(barrier, inc=1, device_id=(b, lax.rem(s + i, NS)), device_id_type=MESH)
        return carry

    def greet_brick(i, carry):
        pl.semaphore_signal(barrier, inc=1, device_id=(lax.rem(b + i, NB), s), device_id_type=MESH)
        return carry

    lax.fori_loop(1, NS, greet_slab, 0)
    lax.fori_loop(1, NB, greet_brick, 0)
    for device in (onward[3], origin[3]):
        pl.semaphore_signal(barrier, inc=1, device_id=device, device_id_type=MESH)

    sources = (
        table_any, first_any, second_any, third_any, e_in_any, w_in_any,
        neigh_any, pos_any, typ_any, count_any,
        e_hid_any, w_hid_any, e_out_any, w_out_any, base_any,
        cx_any, cy_any, cz_any, frac_any, high_any, low_any, twist_any,
    )
    targets = (
        table_ref, first_ref, second_ref, third_ref, e_in_ref, w_in_ref,
        neigh_ref, pos_ref, typ_ref, count_ref,
        e_hid_ref, w_hid_ref, e_out_ref, w_out_ref, base_ref,
        cx_ref.at[0], cy_ref.at[0], cz_ref.at[0], frac_ref.at[0], high_ref, low_ref, twist_ref,
    )
    loads = [
        pltpu.make_async_copy(source, target, load_sem.at[i])
        for i, (source, target) in enumerate(zip(sources, targets, strict=True))
    ]
    for load in loads:
        load.start()

    pl.semaphore_wait(barrier, NS + NB)

    def remote(source, target, send_sem, recv_sem, device):
        return pltpu.make_async_remote_copy(
            src_ref=source, dst_ref=target, send_sem=send_sem, recv_sem=recv_sem,
            device_id=device, device_id_type=MESH,
        )

    plan = (
        (above, pos_any, low_pos), (above, typ_any, low_typ), (above, snd_any, low_snd),
        (below, pos_any, upp_pos), (below, typ_any, upp_typ), (below, snd_any, upp_snd),
    )
    ghosts = [
        remote(source, target, ghost_send.at[i], ghost_recv.at[i], device)
        for i, (device, source, target) in enumerate(plan)
    ]
    for ghost in ghosts:
        ghost.start()
    cells = []
    for n in range(1, 4):
        pairs = ((cx_any, cx_ref), (cy_any, cy_ref), (cz_any, cz_ref), (frac_any, frac_ref))
        for i, (source, target) in enumerate(pairs):
            k = (n - 1) * 4 + i
            cells.append(
                remote(source, target.at[n], cell_send.at[k], cell_recv.at[k], onward[n])
            )
    for cell in cells:
        cell.start()

    row = rows_iota((256, 128))
    lane = lanes_iota((256, 128))

    def kappa(index):
        folded = jnp.minimum(index, NG - index)
        return folded.astype(F32) * (2.0 * math.pi / NG)

    kx = kappa(row // 8 + 32 * (lane // 16))
    ky = kappa(b * 8 + row % 8)
    kz = kappa(s * 16 + lane % 16)
    squared = kx * kx + ky * ky + kz * kz
    root = jnp.where(squared == 0.0, 1.0, 0.0)
    green_ref[...] = (1.0 - root) * jnp.exp(-0.5 * squared) / (squared + root) * (1.0 / NG)

    for load in loads[:4]:
        load.wait()
    f1 = lax.dot_general(table_ref[0:32, 0:25], first_ref[...], NT, precision=HIGHEST)
    oxygen, hydrogen = f1[:, 0:1], f1[:, 1:2]
    w2 = lax.dot_general(table_ref[32:96, 0:50], second_ref[...], NT, precision=HIGHEST)
    w2 = lax.dot_general(w2, table_ref[208:233, 0:96], NN, precision=HIGHEST)
    high, low = halves(w2)
    slot = lanes_iota((64, 96)) // 32
    w2_ref[...] = jnp.where(slot == 1, low.astype(F32), high.astype(F32)).astype(BF16)
    w3 = lax.dot_general(table_ref[96:208, 0:100], third_ref[...], NT, precision=HIGHEST)
    w3 = lax.dot_general(w3, table_ref[240:290, 0:192], NN, precision=HIGHEST)
    high, low = halves(w3)
    slot = lanes_iota((112, 192)) // 64
    w3_ref[...] = jnp.where(slot == 1, low.astype(F32), high.astype(F32)).astype(BF16)

    for load in loads[4:10]:
        load.wait()
    high, low = halves(e_in_ref[...])
    in_h_ref[0:240, :] = high
    in_l_ref[0:240, :] = low
    high, low = halves(w_in_ref[...])
    in_h_ref[240:480, :] = high
    in_l_ref[240:480, :] = low

    n = jnp.concatenate(
        [
            neigh_ref[0, :, 0:128],
            jnp.concatenate([neigh_ref[0, 0:32, 128:192], neigh_ref[0, 32:64, 128:192]], axis=1),
        ],
        axis=0,
    )

    def near(row):
        return row[:, 0:128]

    def far(row):
        return jnp.concatenate([row[:, 128:192], row[:, 128:192]], axis=1)

    def by_atom(row):
        return jnp.concatenate(
            [jnp.broadcast_to(near(row), (64, 128)), jnp.broadcast_to(far(row), (32, 128))], axis=0
        )

    own_index = (n - 96) & 127
    lower_index = n & 127
    upper_index = (n - 288) & 127
    row96 = rows_iota((96, 128))
    slot = jnp.where(row96 < 64, row96, row96 - 64 + jnp.where(lanes_iota((96, 128)) < 64, 0, 32))
    live = slot < by_atom(count_ref[...])

    for ghost in ghosts:
        ghost.wait_recv()

    low_snd_row = low_snd[...]
    upp_snd_row = upp_snd[...]
    low_list = jnp.concatenate([low_snd_row[:, 96:192], low_snd_row[:, 0:32]], axis=1)
    upp_list = upp_snd_row[:, 0:128]

    def ghost_row(row, index):
        index = jnp.broadcast_to(index, (8, 128))
        value = jnp.where(index < 128, pick(near(row), index & 127), pick(far(row), index & 127))
        return value[0:1]

    gathered = []
    for c in range(4):
        own = pos_ref[c] if c < 3 else typ_ref[...].astype(F32)
        low = low_pos[c] if c < 3 else low_typ[...].astype(F32)
        upp = upp_pos[c] if c < 3 else upp_typ[...].astype(F32)
        value = jnp.where(n < 224, pick(near(own), own_index), pick(far(own), own_index))
        value = jnp.where(n < 96, pick(ghost_row(low, low_list), lower_index), value)
        value = jnp.where(n >= 288, pick(ghost_row(upp, upp_list), upper_index), value)
        if c < 3:
            value = value - by_atom(own)
        gathered.append(value)
    squared = gathered[0] * gathered[0] + gathered[1] * gathered[1] + gathered[2] * gathered[2]
    smooth = jnp.where(live, 1.0 / (1.0 + squared), 0.0)
    env_ref[0] = smooth
    for c in range(3):
        env_ref[c + 1] = smooth * gathered[c]
    env_ref[4] = gathered[3]
    moment_ref[...] = jnp.zeros_like(moment_ref)

    oxygen_wide = jnp.broadcast_to(oxygen, (32, 128))
    hydrogen_wide = jnp.broadcast_to(hydrogen, (32, 128))

    def chunk(step, carry):
        at = pl.multiple_of(step * 8, 8)
        tile = step // 8
        first = []
        for r in range(8):
            sm = env_ref[0, pl.ds(at + r, 1), :]
            kind = env_ref[4, pl.ds(at + r, 1), :]
            mixing = jnp.where(kind > 0.5, hydrogen_wide, oxygen_wide)
            first.append(jnp.tanh(sm * mixing))
        first = jnp.concatenate(first, axis=1)
        high, low = halves(first)
        second = dot(w2_ref[...], jnp.concatenate([high, high, low], axis=0))
        second = jnp.tanh(second[:56]) + jnp.concatenate([first[:24], first], axis=0)
        padded = jnp.concatenate([second, jnp.zeros((8, 1024), F32)], axis=0)
        high, low = halves(padded)
        third = dot(w3_ref[...], jnp.concatenate([high, high, low], axis=0))
        third = jnp.tanh(third[:104]) + jnp.concatenate([second[:48], second], axis=0)
        for c in range(4):
            total = None
            for r in range(8):
                part = third[:, r * 128 : (r + 1) * 128] * env_ref[c, pl.ds(at + r, 1), :]
                total = part if total is None else total + part
            moment_ref[tile, c] += total
        return carry

    lax.fori_loop(0, 12, chunk, 0)

    for c in range(4):
        moment_ref[0, c] = moment_ref[0, c] * (1.0 / 64.0)
        value = moment_ref[1, c]
        moment_ref[1, c] = (value + pltpu.roll(value, 64, 1)) * (1.0 / 64.0)
    for tile in range(2):
        factors = [moment_ref[tile, c, 0:16, :] for c in range(4)]
        for m, place in enumerate(places()):
            value = None
            for c in range(4):
                term = moment_ref[tile, c, place : place + 1, :] * factors[c]
                value = term if value is None else value + term
            high, low = halves(value)
            desc_h_ref[m * 16 : m * 16 + 16, tile * 128 : (tile + 1) * 128] = high
            desc_l_ref[m * 16 : m * 16 + 16, tile * 128 : (tile + 1) * 128] = low

    both = jnp.tanh(dot3((in_h_ref[...], in_l_ref[...]), (desc_h_ref[...], desc_l_ref[...])))
    for load in loads[10:]:
        load.wait()

    def network(hidden, hid_ref, out_ref):
        for layer in range(2):
            hidden = jnp.tanh(dot3(halves(hidden), halves(hid_ref[layer]))) + hidden
        row = jnp.broadcast_to(out_ref[...], (16, 240))
        return dot3(halves(row), halves(hidden), NT)[0:1, 0:A]

    energy = network(both[:240].T, e_hid_ref, e_out_ref)
    shift = network(both[240:].T, w_hid_ref, w_out_ref)
    charge = jnp.where(typ_ref[...] == 1, base_ref[0:1, 1:2], base_ref[0:1, 0:1]) + shift
    charge_ref[...] = charge
    charges = [
        remote(charge_ref, charges_ref.at[n], charge_send.at[n], charge_recv.at[n], onward[n])
        for n in range(1, 4)
    ]
    for copy in charges:
        copy.start()

    for cell in cells:
        cell.wait_recv()
    grid = None
    for n, (dx, dy) in enumerate(shifts):
        wx = place_rows(cx_ref[n] - dx * CX, spline_rows(frac_ref[n, 0]), CX, 0)
        wy = place_rows(cy_ref[n] - dy * CY, spline_rows(frac_ref[n, 1]), CY, 0)
        high, low = halves(place_rows(cz_ref[n], spline_rows(frac_ref[n, 2]), NG, NG))
        wz_h_ref[n] = high
        wz_l_ref[n] = low
        wxy = jnp.concatenate([wx[x : x + 1] * wy for x in range(CX)], axis=0)
        wxy_ref[n] = wxy
    for n in range(4):
        if n:
            charges[n - 1].wait_recv()
        weighted = wxy_ref[n] * (charges_ref[n] if n else charge)
        part = dot3(halves(weighted), (wz_h_ref[n], wz_l_ref[n]), NT)
        grid = part if grid is None else grid + part

    def table(k, count=1):
        at = slice(k * NG, (k + count) * NG)
        return high_ref[at, :], low_ref[at, :]

    spectrum = dot3(halves(grid), table(0))
    chunk_lane = lanes_iota((CY, 128)) // 16
    for to in range(NS):
        tile, chunk_from = divmod(to, 8)
        out = jnp.zeros((CY, 128), F32)
        for x in range(CX):
            source = spectrum[x * CY : (x + 1) * CY, tile * 128 : (tile + 1) * 128]
            shift_by = 16 * (x - chunk_from) % 128
            if shift_by:
                source = pltpu.roll(source, shift_by, 1)
            out = jnp.where(chunk_lane == x, source, out)
        out1[to] = out

    def exchange(source, target, send_sem, recv_sem, me, count, device_of):
        def copy(i):
            to = lax.rem(me + i, count)
            return remote(
                source.at[to], target.at[me], send_sem.at[to], recv_sem.at[me], device_of(to)
            )

        def arrival(i):
            frm = lax.rem(me + count - i, count)
            return remote(
                source.at[frm], target.at[frm], send_sem.at[frm], recv_sem.at[frm], device_of(frm)
            )

        def start(i, carry):
            copy(i).start()
            return carry

        def wait(i, carry):
            arrival(i).wait_recv()
            return carry

        def drain(i, carry):
            copy(i).wait_send()
            return carry

        lax.fori_loop(1, count, start, 0)
        target[me] = source[me]
        lax.fori_loop(1, count, wait, 0)
        return lambda: lax.fori_loop(1, count, drain, 0)

    def over_slab(source, target, send_sem, recv_sem):
        return exchange(source, target, send_sem, recv_sem, s, NS, lambda to: (b, to))

    def over_brick(source, target, send_sem, recv_sem):
        return exchange(source, target, send_sem, recv_sem, b, NB, lambda to: (to, s))

    drains = [over_slab(out1, in1, send1, recv1)]
    data = halves(in1[...].reshape(NG, 128))
    out2[...] = dot3_narrow(table(1), data).reshape(NB, 8, 128)
    drains.append(over_brick(out2, in2, send2, recv2))

    data = halves(in2[...].reshape(NG, 128))
    both = dot3_narrow(table(2, 2), data)
    uc, us = both[:256], both[256:]
    tc, ts = twist_ref[0:256, :], twist_ref[256:512, :]
    turned = jnp.concatenate([uc * tc - us * ts, -(uc * ts + us * tc)], axis=1)
    green = green_ref[...]
    modes = dot3(halves(turned), table(4)) * jnp.concatenate([green, green], axis=1)
    back = dot3(halves(modes), table(4), NT)
    vr, vi = back[:, :128], back[:, 128:]
    real = dot3_narrow(table(2), halves(vr * tc - vi * ts))
    imag = dot3_narrow(table(3), halves(vr * ts + vi * tc))
    out3[...] = (real - imag).reshape(NB, 8, 128)
    drains.append(over_brick(out3, in3, send3, recv3))
    data = halves(in3[...].reshape(NG, 128))
    out4[...] = dot3_narrow(table(0), data).reshape(NS, CY, 128)
    drains.append(over_slab(out4, in4, send4, recv4))

    for x in range(CX):
        for tile in range(2):
            out = jnp.zeros((CY, 128), F32)
            for c in range(8):
                source = in4[8 * tile + c]
                shift_by = 16 * (c - x) % 128
                if shift_by:
                    source = pltpu.roll(source, shift_by, 1)
                out = jnp.where(chunk_lane == c, source, out)
            modes_ref[x * CY : (x + 1) * CY, tile * 128 : (tile + 1) * 128] = out
    potential = dot3(halves(modes_ref[...]), table(0), NT)
    pot_ref[...] = potential.reshape(CX, CY, NG)
    pot_copy = pltpu.make_async_copy(pot_ref, pot_any, pot_sem)
    pot_copy.start()

    data = halves(potential)
    returns = []
    for n in (1, 2, 3, 0):
        sampled = dot3(data, (wz_h_ref[n], wz_l_ref[n]))
        part_ref[n] = jnp.sum(sampled * wxy_ref[n], axis=0, keepdims=True)
        if n:
            copy = remote(part_ref.at[n], back_ref.at[n], part_send.at[n], part_recv.at[n], origin[n])
            copy.start()
            returns.append(copy)
    for drain in drains:
        drain()
    for copy in ghosts + cells + charges:
        copy.wait_send()
    for copy in returns:
        copy.wait_recv()
    at = part_ref[0] + back_ref[1] + back_ref[2] + back_ref[3]
    energy_ref[...] = energy + 0.5 * charge * at
    for copy in returns:
        copy.wait_send()
    pot_copy.wait()


def hand_over(energy_in, pot_in, energy_out, pot_out, energy_ref, pot_ref, sem):
    arriving = [
        pltpu.make_async_copy(energy_in, energy_ref, sem.at[0]),
        pltpu.make_async_copy(pot_in, pot_ref, sem.at[1]),
    ]
    leaving = [
        pltpu.make_async_copy(energy_ref, energy_out, sem.at[2]),
        pltpu.make_async_copy(pot_ref, pot_out, sem.at[3]),
    ]
    for copy in arriving:
        copy.start()
    for first, second in zip(arriving, leaving, strict=True):
        first.wait()
        second.start()
    for copy in leaving:
        copy.wait()


VMEM = pl.BlockSpec(memory_space=pltpu.VMEM)
ANY = pl.BlockSpec(memory_space=pl.ANY)
I32 = jnp.int32


def per_device(
    positions, types, neighbours, neighbour_count, send_index, cell_x, cell_y, cell_z, spline_fraction,
    embed_first, embed_second, embed_third, energy_in, energy_hidden, energy_out,
    wannier_in, wannier_hidden, wannier_out, charge_base,
):
    vmem = pltpu.VMEM
    dma = pltpu.SemaphoreType.DMA
    slab_block, brick_block = vmem((NS, CY, 128), F32), vmem((NB, 8, 128), F32)
    outs = (jax.ShapeDtypeStruct((1, A), F32), jax.ShapeDtypeStruct((CX, CY, NG), F32))
    results = tuple(
        pl.pallas_call(
            kernel,
            out_shape=outs,
            in_specs=[ANY] * 23,
            out_specs=(VMEM, ANY),
            scratch_shapes=[
                vmem((3, 1, A), F32), vmem((1, A), I32), vmem((1, 64, A), I32), vmem((1, A), I32),
                vmem((4, 1, A), I32), vmem((4, 1, A), I32), vmem((4, 1, A), I32), vmem((4, 3, 1, A), F32),
                vmem((2, 25), F32), vmem((25, 50), F32), vmem((50, 100), F32),
                vmem((240, 1600), F32), vmem((2, 240, 240), F32), vmem((1, 240), F32),
                vmem((240, 1600), F32), vmem((2, 240, 240), F32), vmem((1, 240), F32),
                vmem((1, 2), F32), vmem((296, 256), F32),
                vmem((5 * NG, NG), BF16), vmem((5 * NG, NG), BF16), vmem((2 * NG, 128), F32),
                vmem((3, 1, A), F32), vmem((1, A), I32), vmem((1, A), I32),
                vmem((3, 1, A), F32), vmem((1, A), I32), vmem((1, A), I32),
                vmem((5, 96, 128), F32), vmem((2, 4, 104, 128), F32),
                vmem((480, 1600), BF16), vmem((480, 1600), BF16),
                vmem((1600, 256), BF16), vmem((1600, 256), BF16),
                vmem((64, 96), BF16), vmem((112, 192), BF16),
                vmem((1, A), F32), vmem((4, 1, A), F32), vmem((4, 128, A), F32),
                vmem((4, NG, A), BF16), vmem((4, NG, A), BF16), vmem((NG, 128), F32),
                slab_block, slab_block, brick_block, brick_block,
                brick_block, brick_block, slab_block, slab_block,
                vmem((128, NG), F32), vmem((CX, CY, NG), F32), vmem((4, 1, A), F32), vmem((4, 1, A), F32),
                dma((LOADED,)), dma, dma((6,)), dma((6,)), dma((12,)), dma((12,)), dma((4,)), dma((4,)),
                dma((4,)), dma((4,)), dma((NS,)), dma((NS,)), dma((NB,)), dma((NB,)),
                dma((NB,)), dma((NB,)), dma((NS,)), dma((NS,)),
            ],
            compiler_params=pltpu.CompilerParams(
                collective_id=1, has_side_effects=True, vmem_limit_bytes=60 * MIB
            ),
            name="potential",
        )(
            positions, types, send_index, jnp.swapaxes(neighbours, 1, 2), neighbour_count,
            cell_x, cell_y, cell_z, spline_fraction,
            embed_first, embed_second, embed_third,
            energy_in.T, energy_hidden, energy_out.reshape(1, -1),
            wannier_in.T, wannier_hidden, wannier_out.reshape(1, -1), charge_base.reshape(1, 2),
            embedding_tables(), *transform_tables(),
        )
    )
    return pl.pallas_call(
        hand_over,
        out_shape=outs,
        in_specs=[ANY, ANY],
        out_specs=(ANY, ANY),
        scratch_shapes=[vmem((1, A), F32), vmem((CX, CY, NG), F32), dma((4,))],
        compiler_params=pltpu.CompilerParams(vmem_limit_bytes=60 * MIB),
        name="hand_over",
    )(*results)


def solution(mesh):
    row = P("slab", "brick")
    three = P(None, "slab", "brick")
    placed = (three, row, P("slab", "brick", None), row, row, row, row, row, three) + (P(),) * 10
    return jax.shard_map(
        per_device,
        mesh=mesh,
        in_specs=placed,
        out_specs=(row, P("brick", "slab", None)),
        check_vma=False,
    )
```

time: 84.7 us -> 75.9 us (0.90)
  the two profiles are of different devices: /device:TPU:16 before, /device:TPU:1 now
where the time goes in v3:
time: 75.9 us; the launch traced here: 75.4 us
  Pallas kernels  74.7 us (98%)
    pallas_call x1, Pallas kernels, per_device(): pl.pallas_call(kernel, out_shape=outs, in_specs=[ANY] * 23, out_specs=(VM...  73.1 us
    pallas_call x1, Pallas kernels, per_device(): pl.pallas_call(hand_over, out_shape=outs, in_specs=[ANY, ANY], out_specs=...  1.6 us

profile of v3, /device:TPU:1, one launch (start us, length us, event | category | flops | bytes accessed | tf_op | source)
XLA Modules:
  0.0 75.4 jit_solution(680368393849970516)
XLA Ops:
  0.6 73.1 %potential.1 = (f32[1,192]{1,0:T(1,128)}, f32[8,16,256]{2,1,0:T(8,128)}) custom-call(f32[3,1,192]{2,1,0:T(1,128)} %pos_any.1, s32[1,192]{1,0:T(1,128)} %typ_any.1, s32[1,192]{1,0:T(1,128)} %snd_any.1, s32[1,64,192]{2,1,0:T(8,128)} %bitcast.8, s32[1,192]{1,0:T(1,128)} %count_any.1, s32[1,192]{1,0:T(1,128)} %cx_any.1, s32[1,192]{1,0:T(1,128)} %cy_any.1, ...), custom_call_target="tpu_custom_call" | custom-call | tf_op jit(solution)/shard_map/potential/pallas_call | solution.py:571
  73.8 1.6 %hand_over.1 = (f32[1,192]{1,0:T(1,128)}, f32[8,16,256]{2,1,0:T(8,128)}) custom-call(f32[1,192]{1,0:T(1,128)} %get-tuple-element.4.energy_in, f32[8,16,256]{2,1,0:T(8,128)} %get-tuple-element.5.pot_in), custom_call_target="tpu_custom_call" | custom-call | tf_op jit(solution)/shard_map/hand_over/pallas_call | solution.py:612

commit v4 on v3

--- a/solution.py
+++ b/solution.py
@@ -367,7 +367,7 @@
             moment_ref[tile, c] += total
         return carry
 
-    lax.fori_loop(0, 12, chunk, 0)
+    lax.fori_loop(0, 12, chunk, 0, unroll=4)
 
     for c in range(4):
         moment_ref[0, c] = moment_ref[0, c] * (1.0 / 64.0)
@@ -384,18 +384,21 @@
             desc_h_ref[m * 16 : m * 16 + 16, tile * 128 : (tile + 1) * 128] = high
             desc_l_ref[m * 16 : m * 16 + 16, tile * 128 : (tile + 1) * 128] = low
 
-    both = jnp.tanh(dot3((in_h_ref[...], in_l_ref[...]), (desc_h_ref[...], desc_l_ref[...])))
     for load in loads[10:]:
         load.wait()
 
-    def network(hidden, hid_ref, out_ref):
+    def network(rows, hid_ref, out_ref):
+        weight = in_h_ref[rows, :], in_l_ref[rows, :]
+        hidden = jnp.tanh(dot3(weight, (desc_h_ref[...], desc_l_ref[...]))).T
         for layer in range(2):
             hidden = jnp.tanh(dot3(halves(hidden), halves(hid_ref[layer]))) + hidden
         row = jnp.broadcast_to(out_ref[...], (16, 240))
         return dot3(halves(row), halves(hidden), NT)[0:1, 0:A]
 
-    energy = network(both[:240].T, e_hid_ref, e_out_ref)
-    shift = network(both[240:].T, w_hid_ref, w_out_ref)
+    def short_energy():
+        energy_ref[...] = network(slice(0, 240), e_hid_ref, e_out_ref)
+
+    shift = network(slice(240, 480), w_hid_ref, w_out_ref)
     charge = jnp.where(typ_ref[...] == 1, base_ref[0:1, 1:2], base_ref[0:1, 0:1]) + shift
     charge_ref[...] = charge
     charges = [
@@ -440,7 +443,7 @@
             out = jnp.where(chunk_lane == x, source, out)
         out1[to] = out
 
-    def exchange(source, target, send_sem, recv_sem, me, count, device_of):
+    def exchange(source, target, send_sem, recv_sem, me, count, device_of, meanwhile=None):
         def copy(i):
             to = lax.rem(me + i, count)
             return remote(
@@ -467,16 +470,18 @@
 
         lax.fori_loop(1, count, start, 0)
         target[me] = source[me]
+        if meanwhile is not None:
+            meanwhile()
         lax.fori_loop(1, count, wait, 0)
         return lambda: lax.fori_loop(1, count, drain, 0)
 
-    def over_slab(source, target, send_sem, recv_sem):
-        return exchange(source, target, send_sem, recv_sem, s, NS, lambda to: (b, to))
+    def over_slab(source, target, send_sem, recv_sem, meanwhile=None):
+        return exchange(source, target, send_sem, recv_sem, s, NS, lambda to: (b, to), meanwhile)
 
     def over_brick(source, target, send_sem, recv_sem):
         return exchange(source, target, send_sem, recv_sem, b, NB, lambda to: (to, s))
 
-    drains = [over_slab(out1, in1, send1, recv1)]
+    drains = [over_slab(out1, in1, send1, recv1, short_energy)]
     data = halves(in1[...].reshape(NG, 128))
     out2[...] = dot3_narrow(table(1), data).reshape(NB, 8, 128)
     drains.append(over_brick(out2, in2, send2, recv2))
@@ -529,7 +534,7 @@
     for copy in returns:
         copy.wait_recv()
     at = part_ref[0] + back_ref[1] + back_ref[2] + back_ref[3]
-    energy_ref[...] = energy + 0.5 * charge * at
+    energy_ref[...] += 0.5 * charge_ref[...] * at
     for copy in returns:
         copy.wait_send()
     pot_copy.wait()

time: 75.9 us -> 72.6 us (0.957)
  Pallas kernels: 74.7 us -> 71.5 us
    pallas_call x1, Pallas kernels: 73.1 us -> 69.9 us  [per_device(): pl.pallas_call(kernel, out_shape=outs, in_specs=[ANY] * 23, out_specs=(VM...]
where the time goes in v4:
time: 72.6 us; the launch traced here: 72.1 us
  Pallas kernels  71.5 us (98%)
    pallas_call x1, Pallas kernels, per_device(): pl.pallas_call(kernel, out_shape=outs, in_specs=[ANY] * 23, out_specs=(VM...  69.9 us
    pallas_call x1, Pallas kernels, per_device(): pl.pallas_call(hand_over, out_shape=outs, in_specs=[ANY, ANY], out_specs=...  1.6 us

profile of v4, /device:TPU:1, one launch (start us, length us, event | category | flops | bytes accessed | tf_op | source)
XLA Modules:
  0.0 72.1 jit_solution(5721527127252674934)
XLA Ops:
  0.6 69.9 %potential.1 = (f32[1,192]{1,0:T(1,128)}, f32[8,16,256]{2,1,0:T(8,128)}) custom-call(f32[3,1,192]{2,1,0:T(1,128)} %pos_any.1, s32[1,192]{1,0:T(1,128)} %typ_any.1, s32[1,192]{1,0:T(1,128)} %snd_any.1, s32[1,64,192]{2,1,0:T(8,128)} %bitcast.8, s32[1,192]{1,0:T(1,128)} %count_any.1, s32[1,192]{1,0:T(1,128)} %cx_any.1, s32[1,192]{1,0:T(1,128)} %cy_any.1, ...), custom_call_target="tpu_custom_call" | custom-call | tf_op jit(solution)/shard_map/potential/pallas_call | solution.py:576
  70.5 1.6 %hand_over.1 = (f32[1,192]{1,0:T(1,128)}, f32[8,16,256]{2,1,0:T(8,128)}) custom-call(f32[1,192]{1,0:T(1,128)} %get-tuple-element.4.energy_in, f32[8,16,256]{2,1,0:T(8,128)} %get-tuple-element.5.pot_in), custom_call_target="tpu_custom_call" | custom-call | tf_op jit(solution)/shard_map/hand_over/pallas_call | solution.py:617

commit v5 on v4

--- a/solution.py
+++ b/solution.py
@@ -405,7 +405,7 @@
         remote(charge_ref, charges_ref.at[n], charge_send.at[n], charge_recv.at[n], onward[n])
         for n in range(1, 4)
     ]
-    for copy in charges:
+    for copy in reversed(charges):
         copy.start()
 
     for cell in cells:
@@ -443,48 +443,40 @@
             out = jnp.where(chunk_lane == x, source, out)
         out1[to] = out
 
-    def exchange(source, target, send_sem, recv_sem, me, count, device_of, meanwhile=None):
-        def copy(i):
-            to = lax.rem(me + i, count)
-            return remote(
-                source.at[to], target.at[me], send_sem.at[to], recv_sem.at[me], device_of(to)
-            )
-
-        def arrival(i):
-            frm = lax.rem(me + count - i, count)
-            return remote(
-                source.at[frm], target.at[frm], send_sem.at[frm], recv_sem.at[frm], device_of(frm)
-            )
-
-        def start(i, carry):
-            copy(i).start()
-            return carry
-
-        def wait(i, carry):
-            arrival(i).wait_recv()
-            return carry
-
-        def drain(i, carry):
-            copy(i).wait_send()
-            return carry
-
-        lax.fori_loop(1, count, start, 0)
+    def exchange(source, target, send_sem, recv_sem, me, peers, device_of, meanwhile=None):
+        copies = [
+            remote(source.at[k], target.at[me], send_sem.at[k], recv_sem.at[me], device_of(k))
+            for k in peers
+        ]
+        for copy in copies:
+            copy.start()
         target[me] = source[me]
         if meanwhile is not None:
             meanwhile()
-        lax.fori_loop(1, count, wait, 0)
-        return lambda: lax.fori_loop(1, count, drain, 0)
+        for k in peers:
+            remote(
+                source.at[k], target.at[k], send_sem.at[k], recv_sem.at[k], device_of(k)
+            ).wait_recv()
+        return copies
+
+    far_first = (4, 5, 3, 6, 2, 7, 1)
+    turns = [(1, d) for d in (*far_first, 0)] + [(0, d) for d in far_first]
+    slabs = [lax.rem(s // 8 + half, 2) * 8 + lax.rem(s + d, 8) for half, d in turns]
+    turns = [(x, d) for x in (2, 1, 3) for d in (*far_first, 0)] + [(0, d) for d in far_first]
+    bricks = [lax.rem(b // 8 + x, 4) * 8 + lax.rem(b + d, 8) for x, d in turns]
 
     def over_slab(source, target, send_sem, recv_sem, meanwhile=None):
-        return exchange(source, target, send_sem, recv_sem, s, NS, lambda to: (b, to), meanwhile)
+        return exchange(
+            source, target, send_sem, recv_sem, s, slabs, lambda to: (b, to), meanwhile
+        )
 
     def over_brick(source, target, send_sem, recv_sem):
-        return exchange(source, target, send_sem, recv_sem, b, NB, lambda to: (to, s))
-
-    drains = [over_slab(out1, in1, send1, recv1, short_energy)]
+        return exchange(source, target, send_sem, recv_sem, b, bricks, lambda to: (to, s))
+
+    sent = over_slab(out1, in1, send1, recv1, short_energy)
     data = halves(in1[...].reshape(NG, 128))
     out2[...] = dot3_narrow(table(1), data).reshape(NB, 8, 128)
-    drains.append(over_brick(out2, in2, send2, recv2))
+    sent += over_brick(out2, in2, send2, recv2)
 
     data = halves(in2[...].reshape(NG, 128))
     both = dot3_narrow(table(2, 2), data)
@@ -498,10 +490,10 @@
     real = dot3_narrow(table(2), halves(vr * tc - vi * ts))
     imag = dot3_narrow(table(3), halves(vr * ts + vi * tc))
     out3[...] = (real - imag).reshape(NB, 8, 128)
-    drains.append(over_brick(out3, in3, send3, recv3))
+    sent += over_brick(out3, in3, send3, recv3)
     data = halves(in3[...].reshape(NG, 128))
     out4[...] = dot3_narrow(table(0), data).reshape(NS, CY, 128)
-    drains.append(over_slab(out4, in4, send4, recv4))
+    sent += over_slab(out4, in4, send4, recv4)
 
     for x in range(CX):
         for tile in range(2):
@@ -520,16 +512,14 @@
 
     data = halves(potential)
     returns = []
-    for n in (1, 2, 3, 0):
+    for n in (3, 1, 2, 0):
         sampled = dot3(data, (wz_h_ref[n], wz_l_ref[n]))
         part_ref[n] = jnp.sum(sampled * wxy_ref[n], axis=0, keepdims=True)
         if n:
             copy = remote(part_ref.at[n], back_ref.at[n], part_send.at[n], part_recv.at[n], origin[n])
             copy.start()
             returns.append(copy)
-    for drain in drains:
-        drain()
-    for copy in ghosts + cells + charges:
+    for copy in sent + ghosts + cells + charges:
         copy.wait_send()
     for copy in returns:
         copy.wait_recv()

time: 72.6 us -> 71.5 us (0.985)
  Pallas kernels: 71.5 us -> 70.7 us
    pallas_call x1, Pallas kernels: 69.9 us -> 69.1 us  [per_device(): pl.pallas_call(kernel, out_shape=outs, in_specs=[ANY] * 23, out_specs=(VM...]
where the time goes in v5:
time: 71.5 us; the launch traced here: 71.3 us
  Pallas kernels  70.7 us (99%)
    pallas_call x1, Pallas kernels, per_device(): pl.pallas_call(kernel, out_shape=outs, in_specs=[ANY] * 23, out_specs=(VM...  69.1 us
    pallas_call x1, Pallas kernels, per_device(): pl.pallas_call(hand_over, out_shape=outs, in_specs=[ANY, ANY], out_specs=...  1.6 us

profile of v5, /device:TPU:1, one launch (start us, length us, event | category | flops | bytes accessed | tf_op | source)
XLA Modules:
  0.0 71.3 jit_solution(13620756513466375930)
XLA Ops:
  0.6 69.1 %potential.1 = (f32[1,192]{1,0:T(1,128)}, f32[8,16,256]{2,1,0:T(8,128)}) custom-call(f32[3,1,192]{2,1,0:T(1,128)} %pos_any.1, s32[1,192]{1,0:T(1,128)} %typ_any.1, s32[1,192]{1,0:T(1,128)} %snd_any.1, s32[1,64,192]{2,1,0:T(8,128)} %bitcast.8, s32[1,192]{1,0:T(1,128)} %count_any.1, s32[1,192]{1,0:T(1,128)} %cx_any.1, s32[1,192]{1,0:T(1,128)} %cy_any.1, ...), custom_call_target="tpu_custom_call" | custom-call | tf_op jit(solution)/shard_map/potential/pallas_call | solution.py:566
  69.7 1.6 %hand_over.1 = (f32[1,192]{1,0:T(1,128)}, f32[8,16,256]{2,1,0:T(8,128)}) custom-call(f32[1,192]{1,0:T(1,128)} %get-tuple-element.4.energy_in, f32[8,16,256]{2,1,0:T(8,128)} %get-tuple-element.5.pot_in), custom_call_target="tpu_custom_call" | custom-call | tf_op jit(solution)/shard_map/hand_over/pallas_call | solution.py:607

commit v6 on v5

--- a/solution.py
+++ b/solution.py
@@ -196,14 +196,14 @@
         pl.semaphore_signal(barrier, inc=1, device_id=device, device_id_type=MESH)
 
     sources = (
-        table_any, first_any, second_any, third_any, e_in_any, w_in_any,
-        neigh_any, pos_any, typ_any, count_any,
+        table_any, first_any, second_any, third_any, w_in_any,
+        neigh_any, pos_any, typ_any, count_any, e_in_any,
         e_hid_any, w_hid_any, e_out_any, w_out_any, base_any,
         cx_any, cy_any, cz_any, frac_any, high_any, low_any, twist_any,
     )
     targets = (
-        table_ref, first_ref, second_ref, third_ref, e_in_ref, w_in_ref,
-        neigh_ref, pos_ref, typ_ref, count_ref,
+        table_ref, first_ref, second_ref, third_ref, w_in_ref,
+        neigh_ref, pos_ref, typ_ref, count_ref, e_in_ref,
         e_hid_ref, w_hid_ref, e_out_ref, w_out_ref, base_ref,
         cx_ref.at[0], cy_ref.at[0], cz_ref.at[0], frac_ref.at[0], high_ref, low_ref, twist_ref,
     )
@@ -272,11 +272,8 @@
     slot = lanes_iota((112, 192)) // 64
     w3_ref[...] = jnp.where(slot == 1, low.astype(F32), high.astype(F32)).astype(BF16)
 
-    for load in loads[4:10]:
+    for load in loads[4:9]:
         load.wait()
-    high, low = halves(e_in_ref[...])
-    in_h_ref[0:240, :] = high
-    in_l_ref[0:240, :] = low
     high, low = halves(w_in_ref[...])
     in_h_ref[240:480, :] = high
     in_l_ref[240:480, :] = low
@@ -396,6 +393,10 @@
         return dot3(halves(row), halves(hidden), NT)[0:1, 0:A]
 
     def short_energy():
+        loads[9].wait()
+        high, low = halves(e_in_ref[...])
+        in_h_ref[0:240, :] = high
+        in_l_ref[0:240, :] = low
         energy_ref[...] = network(slice(0, 240), e_hid_ref, e_out_ref)
 
     shift = network(slice(240, 480), w_hid_ref, w_out_ref)

time: 71.5 us -> 71.4 us (level)
  no operation moved by 1% of the time
where the time goes in v6:
time: 71.4 us; the launch traced here: 71.3 us
  Pallas kernels  70.7 us (99%)
    pallas_call x1, Pallas kernels, per_device(): pl.pallas_call(kernel, out_shape=outs, in_specs=[ANY] * 23, out_specs=(VM...  69.1 us
    pallas_call x1, Pallas kernels, per_device(): pl.pallas_call(hand_over, out_shape=outs, in_specs=[ANY, ANY], out_specs=...  1.6 us

profile of v6, /device:TPU:1, one launch (start us, length us, event | category | flops | bytes accessed | tf_op | source)
XLA Modules:
  0.0 71.3 jit_solution(6181360595981651157)
XLA Ops:
  0.6 69.1 %potential.1 = (f32[1,192]{1,0:T(1,128)}, f32[8,16,256]{2,1,0:T(8,128)}) custom-call(f32[3,1,192]{2,1,0:T(1,128)} %pos_any.1, s32[1,192]{1,0:T(1,128)} %typ_any.1, s32[1,192]{1,0:T(1,128)} %snd_any.1, s32[1,64,192]{2,1,0:T(8,128)} %bitcast.8, s32[1,192]{1,0:T(1,128)} %count_any.1, s32[1,192]{1,0:T(1,128)} %cx_any.1, s32[1,192]{1,0:T(1,128)} %cy_any.1, ...), custom_call_target="tpu_custom_call" | custom-call | tf_op jit(solution)/shard_map/potential/pallas_call | solution.py:567
  69.7 1.6 %hand_over.1 = (f32[1,192]{1,0:T(1,128)}, f32[8,16,256]{2,1,0:T(8,128)}) custom-call(f32[1,192]{1,0:T(1,128)} %get-tuple-element.4.energy_in, f32[8,16,256]{2,1,0:T(8,128)} %get-tuple-element.5.pot_in), custom_call_target="tpu_custom_call" | custom-call | tf_op jit(solution)/shard_map/hand_over/pallas_call | solution.py:608
